TPU v7x, 32 devices: a whole 2x2x4 slice. The times are simulated.
32 devices in a mesh: dp: 8 (over y, x, core), chan: 4 (over z).
Axes of the slice: x: 2, y: 2, z: 4, core: 2. Of those that a mesh axis runs over, the one named last changes fastest.
Arguments:
- images: bfloat16 [64, 81, 2048], P('dp', None, 'chan'), may hold values from -6 to 6
- groups: int32 [64], P('dp'), may hold values from 0 to 2, as said below
- cotangent: bfloat16 [64, 81, 2048], P('dp', None, 'chan'), may hold values from -6 to 6
- reduce_weight: float32 [512, 2048], P('chan'), may hold values from -0.125 to 0.125
- spatial_weight: float32 [512, 3, 3, 512], P('chan'), may hold values from -0.09375 to 0.09375
- expand_weight: float32 [512, 2048], P('chan'), may hold values from -0.25 to 0.25
- inner_norm: float32 [2, 2, 512], P(None, None, 'chan')
- outer_norm: float32 [2, 2048], P(None, 'chan')
- reduce_moments: float32 [2, 512, 2048], P(None, 'chan'), as said below
- spatial_moments: float32 [2, 512, 3, 3, 512], P(None, 'chan')
- expand_moments: float32 [2, 512, 2048], P(None, 'chan')
- inner_moments: float32 [2, 2, 2, 512], P(None, None, None, 'chan')
- outer_moments: float32 [2, 2, 2048], P(None, None, 'chan')
- reduce_ema: float32 [512, 2048], P('chan'), may hold values from -0.125 to 0.125
- spatial_ema: float32 [512, 3, 3, 512], P('chan'), may hold values from -0.09375 to 0.09375
- expand_ema: float32 [512, 2048], P('chan'), may hold values from -0.25 to 0.25
- inner_ema: float32 [2, 2, 512], P(None, None, 'chan')
- outer_ema: float32 [2, 2048], P(None, 'chan')
Outputs:
- output: float32 [64, 81, 2048], P('dp', None, 'chan')
- input_grad: float32 [64, 81, 2048], P('dp', None, 'chan')
- new_reduce_weight: float32 [512, 2048], P('chan')
- new_reduce_first: float32 [512, 2048], P('chan')
- new_reduce_second: float32 [512, 2048], P('chan')
- new_reduce_ema: float32 [512, 2048], P('chan')
- new_spatial_weight: float32 [512, 3, 3, 512], P('chan')
- new_spatial_first: float32 [512, 3, 3, 512], P('chan')
- new_spatial_second: float32 [512, 3, 3, 512], P('chan')
- new_spatial_ema: float32 [512, 3, 3, 512], P('chan')
- new_expand_weight: float32 [512, 2048], P('chan')
- new_expand_first: float32 [512, 2048], P('chan')
- new_expand_second: float32 [512, 2048], P('chan')
- new_expand_ema: float32 [512, 2048], P('chan')
- new_inner_norm: float32 [2, 2, 512], P(None, None, 'chan')
- new_inner_first: float32 [2, 2, 512], P(None, None, 'chan')
- new_inner_second: float32 [2, 2, 512], P(None, None, 'chan')
- new_inner_ema: float32 [2, 2, 512], P(None, None, 'chan')
- new_outer_norm: float32 [2, 2048], P(None, 'chan')
- new_outer_first: float32 [2, 2048], P(None, 'chan')
- new_outer_second: float32 [2, 2048], P(None, 'chan')
- new_outer_ema: float32 [2, 2048], P(None, 'chan')
Inputs may be any that keep to these rules, and one draw needn't show every extreme that they name: `groups`: group g means a (5 + 2g) x (5 + 2g) image in the top-left corner of its 9 x 9 grid; the first image is of group 0 and the last of group 2. `reduce_moments`: second moments are positive.
All inputs are finite; a program needn't handle non-finite values.
Results may differ from a plain program's by a relative error of at most 0.023.
Values may be sent and summed in bfloat16 or wider, within the bound.
A program may use at most 128 MiB of HBM per device.

v0:
```python
import math

import jax
import jax.numpy as jnp
from jax import lax
from jax.sharding import PartitionSpec as P

MAP = 9
STEP = 5


norm_eps = 1e-05
adam_eps = 1e-08
beta_one = 0.5
beta_two = 0.5
decay_rate = 0.05
ema_rate = 0.75
norm_rate = 0.3


def pixel_mask(groups):
    side = 5 + 2 * groups
    place = jnp.arange(MAP * MAP, dtype=jnp.int32)
    inside = ((place // MAP)[None, :] < side[:, None]) & ((place % MAP)[None, :] < side[:, None])
    return inside.astype(jnp.float32).reshape(-1, 1)


def silu_slope(values):
    sigma = jax.nn.sigmoid(values)
    return sigma * (1.0 + values * (1.0 - sigma))


def unfold(acts, count_img):
    channels = acts.shape[-1]
    grid = acts.reshape(count_img, MAP, MAP, channels)
    padded = jnp.pad(grid, ((0, 0), (1, 1), (1, 1), (0, 0)))
    pieces = [
        padded[:, vertical : vertical + MAP, lateral : lateral + MAP, :]
        for vertical in range(3)
        for lateral in range(3)
    ]
    return jnp.concatenate(pieces, axis=-1).reshape(count_img * MAP * MAP, 9 * channels)


def fold_columns(column_grad, count_img, channels):
    grid = column_grad.reshape(count_img, MAP, MAP, 9, channels)
    total = jnp.zeros((count_img, MAP + 2, MAP + 2, channels), jnp.float32)
    for vertical in range(3):
        for lateral in range(3):
            piece = grid[:, :, :, vertical * 3 + lateral, :]
            total = total + jnp.pad(
                piece, ((0, 0), (vertical, 2 - vertical), (lateral, 2 - lateral), (0, 0))
            )
    return total[:, 1 : MAP + 1, 1 : MAP + 1, :].reshape(count_img * MAP * MAP, channels)


def norm_forward(values, mask, gain, bias):
    local_count = jnp.sum(mask)
    totals, count = lax.psum((jnp.sum(values * mask, axis=0), local_count), "dp")
    average = totals / count
    centered = values - average
    variance = lax.psum(jnp.sum(mask * centered * centered, axis=0), "dp") / count
    inverse = lax.rsqrt(variance + norm_eps)
    normed = centered * inverse
    return (gain * normed + bias, normed, inverse, count)


def norm_backward(incoming, normed, inverse, gain, mask, count):
    bias_grad, gain_grad = lax.psum(
        (jnp.sum(incoming, axis=0), jnp.sum(incoming * normed, axis=0)), "dp"
    )
    result = inverse * gain * (incoming - mask * (bias_grad + normed * gain_grad) / count)
    return (result, gain_grad, bias_grad)


def adamw(weight, moments, average, grad, rate, decay):
    first = beta_one * moments[0] + (1.0 - beta_one) * grad
    second = beta_two * moments[1] + (1.0 - beta_two) * grad * grad
    corr_one = 1.0 - beta_one**STEP
    corr_two = 1.0 - beta_two**STEP
    new_weight = weight - rate * (
        first / corr_one / (jnp.sqrt(second / corr_two) + adam_eps) + decay * weight
    )
    new_average = ema_rate * average + (1.0 - ema_rate) * new_weight
    return (new_weight, first, second, new_average)


def per_device(
    images,
    groups,
    cotangent,
    reduce_weight,
    spatial_weight,
    expand_weight,
    inner_norm,
    outer_norm,
    reduce_moments,
    spatial_moments,
    expand_moments,
    inner_moments,
    outer_moments,
    reduce_ema,
    spatial_ema,
    expand_ema,
    inner_ema,
    outer_ema,
):
    count_img, cells, wide_part = images.shape
    rows = count_img * cells
    wide = reduce_weight.shape[1]
    inner = spatial_weight.shape[3]
    inner_part = reduce_weight.shape[0]
    mask = pixel_mask(groups)
    inputs = images.reshape(rows, wide_part).astype(jnp.float32)
    reduce_low = reduce_weight.astype(jnp.bfloat16)
    spatial_low = spatial_weight.astype(jnp.bfloat16).reshape(inner_part, 9 * inner)
    expand_low = expand_weight.astype(jnp.bfloat16)
    piece = lax.all_gather(images, "chan", axis=2, tiled=True)
    block = piece.reshape(rows, piece.shape[2])
    first_pre = jnp.einsum("rc,kc->rk", block, reduce_low, preferred_element_type=jnp.float32)
    first_norm, first_hat, first_inv, count = norm_forward(
        first_pre, mask, inner_norm[0, 0], inner_norm[1, 0]
    )
    first_act = (jax.nn.silu(first_norm) * mask).astype(jnp.bfloat16)
    first_full = lax.all_gather(first_act, "chan", axis=1, tiled=True)
    columns = unfold(first_full, count_img)
    second_pre = jnp.einsum("rt,kt->rk", columns, spatial_low, preferred_element_type=jnp.float32)
    second_norm, second_hat, second_inv, count_two = norm_forward(
        second_pre, mask, inner_norm[0, 1], inner_norm[1, 1]
    )
    second_act = (jax.nn.silu(second_norm) * mask).astype(jnp.bfloat16)
    partial_out = jnp.dot(second_act, expand_low, preferred_element_type=jnp.float32)
    third_pre = lax.psum_scatter(
        partial_out.astype(jnp.bfloat16), "chan", scatter_dimension=1, tiled=True
    ).astype(jnp.float32)
    third_norm, third_hat, third_inv, count_three = norm_forward(
        third_pre, mask, outer_norm[0], outer_norm[1]
    )
    summed = third_norm + inputs
    output = jax.nn.silu(summed) * mask
    out_grad = cotangent.reshape(rows, wide_part).astype(jnp.float32) * silu_slope(summed) * mask
    third_grad, outer_gain_grad, outer_bias_grad = norm_backward(
        out_grad, third_hat, third_inv, outer_norm[0], mask, count
    )
    third_low = third_grad.astype(jnp.bfloat16)
    third_full = lax.all_gather(third_low, "chan", axis=1, tiled=True)
    expand_grad = jnp.einsum(
        "rk,rw->kw", second_act, third_full, preferred_element_type=jnp.float32
    )
    second_act_grad = jnp.einsum(
        "rw,kw->rk", third_full, expand_low, preferred_element_type=jnp.float32
    )
    second_incoming = second_act_grad * silu_slope(second_norm) * mask
    second_grad, second_gain_grad, second_bias_grad = norm_backward(
        second_incoming, second_hat, second_inv, inner_norm[0, 1], mask, count
    )
    second_low = second_grad.astype(jnp.bfloat16)
    spatial_grad = jnp.einsum(
        "rk,rt->kt", second_low, columns, preferred_element_type=jnp.float32
    ).reshape(inner_part, 3, 3, inner)
    column_grad = jnp.einsum(
        "rk,kt->rt", second_low, spatial_low, preferred_element_type=jnp.float32
    )
    first_partial = fold_columns(column_grad, count_img, inner)
    first_act_grad = lax.psum_scatter(
        first_partial.astype(jnp.bfloat16), "chan", scatter_dimension=1, tiled=True
    ).astype(jnp.float32)
    first_incoming = first_act_grad * silu_slope(first_norm) * mask
    first_grad, first_gain_grad, first_bias_grad = norm_backward(
        first_incoming, first_hat, first_inv, inner_norm[0, 0], mask, count
    )
    first_low = first_grad.astype(jnp.bfloat16)
    piece = lax.all_gather(images, "chan", axis=2, tiled=True)
    block = piece.reshape(rows, piece.shape[2])
    reduce_grad = jnp.einsum("rk,rc->kc", first_low, block, preferred_element_type=jnp.float32)
    input_partial = jnp.einsum(
        "rk,kc->rc", first_low, reduce_low, preferred_element_type=jnp.float32
    )
    input_grad = (
        lax.psum_scatter(
            input_partial.astype(jnp.bfloat16), "chan", scatter_dimension=1, tiled=True
        ).astype(jnp.float32)
        + out_grad
    )
    inner_grad = jnp.stack(
        [
            jnp.stack([first_gain_grad, second_gain_grad]),
            jnp.stack([first_bias_grad, second_bias_grad]),
        ]
    )
    outer_grad = jnp.stack([outer_gain_grad, outer_bias_grad])
    reduce_rate = 2.0 / math.sqrt(wide)
    spatial_rate = 2.0 / math.sqrt(9 * inner)
    expand_rate = 2.0 / math.sqrt(inner)
    reduce_total, spatial_total, expand_total = (
        lax.psum(reduce_grad.astype(jnp.bfloat16), "dp").astype(jnp.float32),
        lax.psum(spatial_grad.astype(jnp.bfloat16), "dp").astype(jnp.float32),
        lax.psum(expand_grad.astype(jnp.bfloat16), "dp").astype(jnp.float32),
    )
    new_reduce = adamw(
        reduce_weight, reduce_moments, reduce_ema, reduce_total, reduce_rate, decay_rate
    )
    new_spatial = adamw(
        spatial_weight, spatial_moments, spatial_ema, spatial_total, spatial_rate, decay_rate
    )
    new_expand = adamw(
        expand_weight, expand_moments, expand_ema, expand_total, expand_rate, decay_rate
    )
    new_inner = adamw(inner_norm, inner_moments, inner_ema, inner_grad, norm_rate, 0.0)
    new_outer = adamw(outer_norm, outer_moments, outer_ema, outer_grad, norm_rate, 0.0)
    return (
        output.reshape(count_img, cells, wide_part),
        input_grad.reshape(count_img, cells, wide_part),
        new_reduce[0],
        new_reduce[1],
        new_reduce[2],
        new_reduce[3],
        new_spatial[0],
        new_spatial[1],
        new_spatial[2],
        new_spatial[3],
        new_expand[0],
        new_expand[1],
        new_expand[2],
        new_expand[3],
        new_inner[0],
        new_inner[1],
        new_inner[2],
        new_inner[3],
        new_outer[0],
        new_outer[1],
        new_outer[2],
        new_outer[3],
    )


def solution(mesh):
    placed = (
        P("dp", None, "chan"),
        P("dp"),
        P("dp", None, "chan"),
        P("chan", None),
        P("chan", None, None, None),
        P("chan", None),
        P(None, None, "chan"),
        P(None, "chan"),
        P(None, "chan", None),
        P(None, "chan", None, None, None),
        P(None, "chan", None),
        P(None, None, None, "chan"),
        P(None, None, "chan"),
        P("chan", None),
        P("chan", None, None, None),
        P("chan", None),
        P(None, None, "chan"),
        P(None, "chan"),
    )
    return jax.shard_map(
        per_device,
        mesh=mesh,
        in_specs=placed,
        out_specs=(
            P("dp", None, "chan"),
            P("dp", None, "chan"),
            P("chan", None),
            P("chan", None),
            P("chan", None),
            P("chan", None),
            P("chan", None, None, None),
            P("chan", None, None, None),
            P("chan", None, None, None),
            P("chan", None, None, None),
            P("chan", None),
            P("chan", None),
            P("chan", None),
            P("chan", None),
            P(None, None, "chan"),
            P(None, None, "chan"),
            P(None, None, "chan"),
            P(None, None, "chan"),
            P(None, "chan"),
            P(None, "chan"),
            P(None, "chan"),
            P(None, "chan"),
        ),
        check_vma=False,
    )
```

profile of v0, /device:TPU:0, one launch (start us, length us, event | category | flops | bytes accessed | tf_op | source)
XLA Modules:
  0.0 554.5 jit_solution(17023933858412594130)
XLA Ops:
  8.8 2.7 copy.86
  12.2 55.5 %all-gather.3.cloned.1.call-done = bf16[8,81,2048]{2,0,1:T(8,128)(2,1)} async-done(((bf16[8,81,512]{2,0,1:T(8,128)(2,1)}), bf16[8,81,2048]{2,0,1:T(8,128)(2,1)}) %all-gather.3.cloned.1.call-update) | async-done | bytes 2654224 | tf_op jit(solution)/shard_map/all_gather | solution.py:118
  67.6 4.8 copy.85
  72.5 2.6 reshape.177
  75.1 2.1 multiply_reduce_fusion.3
  77.2 14.3 %all-reduce.13 = (f32[128]{0:T(128)S(1)}, f32[]{:T(128)}) all-reduce(f32[128]{0:T(128)S(1)} %get-tuple-element.179, f32[]{:T(128)} %fusion.32), channel_id=1, replica_groups=mesh['dp'=8,'chan'=4] {'dp'}, use_global_device_ids=true, to_apply=%region_1.2 | all-reduce | flops 129 | bytes 1032 | tf_op jit(solution)/shard_map/psum | solution.py:59
  92.3 11.8 %psum.120 = f32[128]{0:T(128)S(1)} all-reduce(f32[128]{0:T(128)S(1)} %fusion.20), channel_id=1, replica_groups=mesh['dp'=8,'chan'=4] {'dp'}, use_global_device_ids=true, to_apply=%region_5.6 | all-reduce | flops 128 | bytes 1024 | tf_op jit(solution)/shard_map/psum | solution.py:62
  104.1 1.2 fusion.34
  105.4 17.1 %all_gather.11 = bf16[648,512]{1,0:T(8,128)(2,1)} all-gather(bf16[648,128]{1,0:T(8,128)(2,1)S(1)} %multiply_convert_fusion.3), channel_id=1, replica_groups=mesh['dp'=8,'chan'=4] {'chan'}, dimensions={1}, use_global_device_ids=true | all-gather | bytes 829440 | tf_op jit(solution)/shard_map/all_gather | solution.py:125
  122.6 2.2 reshape.178
  124.8 8.6 %pad_slice_fusion = (bf16[8,9,9,512]{3,2,1,0:T(8,128)(2,1)}, bf16[8,9,9,512]{3,2,1,0:T(8,128)(2,1)}, bf16[8,9,9,512]{3,2,1,0:T(8,128)(2,1)}, bf16[8,9,9,512]{3,2...) fusion(bf16[8,9,9,512]{3,2,1,0:T(8,128)(2,1)} %reshape.178), kind=kLoop, calls=%fused_computation.54 | loop fusion | bytes 5971968 | tf_op jit(solution)/shard_map/slice | solution.py:38
  133.3 1.5 concatenate.27
  134.8 2.2 concatenate.21
  137.0 2.2 concatenate.22
  139.2 2.2 concatenate.23
  141.3 2.2 concatenate.24
  143.5 2.2 concatenate.25
  145.7 2.2 concatenate.26
  147.9 2.2 concatenate.20
  150.0 1.3 constant_dynamic-update-slice_fusion.8
  151.3 1.2 constant_dynamic-update-slice_fusion.7
  154.3 1.7 multiply_reduce_fusion.2
  156.5 11.8 %psum.121 = f32[128]{0:T(128)S(1)} all-reduce(f32[128]{0:T(128)S(1)} %get-tuple-element.181), channel_id=1, replica_groups=mesh['dp'=8,'chan'=4] {'dp'}, use_global_device_ids=true, to_apply=%region_7.8 | all-reduce | flops 128 | bytes 1024 | tf_op jit(solution)/shard_map/psum | solution.py:59
  169.1 11.8 %psum.122 = f32[128]{0:T(128)S(1)} all-reduce(f32[128]{0:T(128)S(1)} %fusion.21), channel_id=1, replica_groups=mesh['dp'=8,'chan'=4] {'dp'}, use_global_device_ids=true, to_apply=%region_9.10 | all-reduce | flops 128 | bytes 1024 | tf_op jit(solution)/shard_map/psum | solution.py:62
  180.9 1.2 fusion.33
  182.1 3.7 convolution_convert_fusion.1
  186.0 2.5 copy.87
  188.5 1.3 copy.88
  189.8 2.7 reshape.184
  192.5 2.6 reshape.183
  195.2 40.1 %reduce-scatter.6.cloned.1.call-done = bf16[648,512]{1,0:T(8,128)(2,1)} async-done(((bf16[648,2048]{1,0:T(8,128)(2,1)}), bf16[648,512]{1,0:T(8,128)(2,1)}) %reduce-scatter.6.cloned.1.call-update) | async-done | bytes 663568 | tf_op jit(solution)/shard_map/reduce_scatter | solution.py:133
  235.3 1.3 fusion.14
  236.6 13.4 %psum.123 = f32[512]{0:T(512)S(1)} all-reduce(f32[512]{0:T(512)S(1)} %fusion.14), channel_id=1, replica_groups=mesh['dp'=8,'chan'=4] {'dp'}, use_global_device_ids=true, to_apply=%region_12.13 | all-reduce | flops 512 | bytes 4096 | tf_op jit(solution)/shard_map/psum | solution.py:59
  250.7 1.3 fusion.15
  252.0 11.8 %psum.124 = f32[512]{0:T(512)S(1)} all-reduce(f32[512]{0:T(512)S(1)} %fusion.15), channel_id=1, replica_groups=mesh['dp'=8,'chan'=4] {'dp'}, use_global_device_ids=true, to_apply=%region_14.15 | all-reduce | flops 512 | bytes 4096 | tf_op jit(solution)/shard_map/psum | solution.py:62
  264.5 4.4 fusion.35
  268.9 11.8 %all-reduce.12 = (f32[512]{0:T(512)S(1)}, f32[512]{0:T(512)S(1)}) all-reduce(f32[512]{0:T(512)S(1)} %get-tuple-element.111, f32[512]{0:T(512)S(1)} %get-tuple-element.110), channel_id=1, replica_groups=mesh['dp'=8,'chan'=4] {'dp'}, use_global_device_ids=true, to_apply=%region_18.19 | all-reduce | flops 1024 | bytes 8192 | tf_op jit(solution)/shard_map/psum | solution.py:69
  280.7 3.2 fusion.16
  284.0 53.5 %all-gather.5.cloned.1.call-done = bf16[648,2048]{1,0:T(8,128)(2,1)} async-done(((bf16[648,512]{1,0:T(8,128)(2,1)}), bf16[648,2048]{1,0:T(8,128)(2,1)}) %all-gather.5.cloned.1.call-update) | async-done | bytes 2654224 | tf_op jit(solution)/shard_map/all_gather | solution.py:146
  337.5 3.0 fusion.37
  340.5 13.7 %all-reduce.11 = (f32[128]{0:T(128)S(1)}, f32[128]{0:T(128)S(1)}) all-reduce(f32[128]{0:T(128)S(1)} %get-tuple-element.115, f32[128]{0:T(128)S(1)} %get-tuple-element.114), channel_id=1, replica_groups=mesh['dp'=8,'chan'=4] {'dp'}, use_global_device_ids=true, to_apply=%region_22.23 | all-reduce | flops 256 | bytes 2048 | tf_op jit(solution)/shard_map/psum | solution.py:69
  355.1 11.3 %fusion.22 = f32[8,9,9,9,512]{4,2,3,1,0:T(8,128)} fusion(bf16[9,512,128,1,1]{2,1,0,4,3:T(8,128)(2,1)} %bitcast.123, bf16[8,9,9,128,1]{3,2,1,0,4:T(8,128)(2,1)S(1)} %reshape.185), kind=kOutput, calls=%fused_computation.87 | convolution fusion | flops 764411904 | bytes 13289472 | tf_op jit(solution)/shard_map/rk,kt->rt/dot_general | solution.py:161
  366.4 12.4 %slice_bitcast_fusion.8 = (f32[8,9,9,512]{3,2,1,0:T(8,128)S(1)}, f32[8,9,9,512]{3,2,1,0:T(8,128)S(1)}, f32[8,9,9,512]{3,2,1,0:T(8,128)}, f32[8,9,9,512]{3,2,1,0:...) fusion(f32[8,9,9,9,512]{4,2,3,1,0:T(8,128)} %fusion.22), kind=kLoop, calls=%fused_computation.22 | loop fusion | bytes 23887872 | tf_op jit(solution)/shard_map/squeeze | solution.py:50
  378.8 1.5 pad_add_fusion
  380.3 6.8 %fusion.1 = bf16[8,9,9,512]{3,2,1,0:T(8,128)(2,1)} fusion(f32[8,9,9,512]{3,2,1,0:T(8,128)} %get-tuple-element.162, f32[8,9,9,512]{3,2,1,0:T(8,128)} %get-tuple-element.163, f32[8,9,9,512]{3,2,1,0:T(8,128)S(1)} %get-tuple-element.156, f32[8,9,9,512]{3,2,1,0:T(8,128)} %get-tuple-element.157, f32[8,9,9,512]{3,2,1,0:T(8,128)} %get-tuple-element.158, ...), kind=kLoop, calls=%fused_computation.9 | loop fusion | flops 1990656 | bytes 8626176 | tf_op jit(solution)/shard_map/convert.3
  387.1 1.5 convert_element_type.122
  389.9 9.3 %copy.97 = bf16[4608,648]{1,0:T(8,128)(2,1)} copy(bf16[4608,648]{0,1:T(8,128)(2,1)} %bitcast.120) | data formatting | bytes 11943936 | tf_op jit(solution)/shard_map/rk,rt->kt/dot_general | solution.py:158
  399.2 3.3 convolution_convert_fusion.2
  402.5 6.6 %convolution_convert_fusion.4 = bf16[128,3,3,512]{3,0,2,1:T(8,128)(2,1)} fusion(bf16[3,3,512,648]{3,2,1,0:T(8,128)(2,1)} %bitcast.119, bf16[648,128]{1,0:T(8,128)(2,1)S(1)} %multiply_convert_fusion.1), kind=kOutput, calls=%fused_computation.32 | convolution fusion | flops 765001728 | bytes 7317504 | tf_op jit(solution)/shard_map/rk,rt->kt/dot_general | solution.py:158
  409.0 1.3 reduce-scatter.10.cloned.1.call-done
  411.7 12.5 %all-reduce.10 = (f32[128]{0:T(128)S(1)}, f32[128]{0:T(128)S(1)}) all-reduce(f32[128]{0:T(128)S(1)} %get-tuple-element.113, f32[128]{0:T(128)S(1)} %get-tuple-element.112), channel_id=1, replica_groups=mesh['dp'=8,'chan'=4] {'dp'}, use_global_device_ids=true, to_apply=%region_27.28 | all-reduce | flops 256 | bytes 2048 | tf_op jit(solution)/shard_map/psum | solution.py:69
  425.0 1.5 convolution_convert_fusion.3
  427.7 2.4 convolution_convert_fusion
  430.2 1.6 reshape.180
  431.8 1.8 copy.99
  435.0 52.7 %all-reduce.17.cloned.1.call-done = (bf16[128,2048]{1,0:T(8,128)(2,1)}, bf16[128,3,3,512]{3,0,2,1:T(8,128)(2,1)}, bf16[128,2048]{1,0:T(8,128)(2,1)}) async-done(((bf16[128,2048]{1,0:T(8,128)(2,1)}, bf16[128,3,3,512]{3,0,2,1:T(8,128)(2,1)}, bf16[128,2048]{1,0:T(8,128)(2,1)}), (bf16[128,2048]{1,0:T(8,128)(2,1)}, bf16[128,3,3,512]{3,0,2,1:T(8,128)(2,1)}, ...) | async-done | bytes 2228240 | tf_op jit(solution)/shard_map/psum | solution.py:196
  487.7 4.8 multiply_add_fusion.5
  492.5 2.6 multiply_add_fusion.4
  495.1 1.3 copy-done.4
  497.5 4.7 multiply_add_fusion.1
  502.1 39.8 %reduce-scatter.8.cloned.1.call-done = bf16[648,512]{1,0:T(8,128)(2,1)} async-done(((bf16[648,2048]{1,0:T(8,128)(2,1)}), bf16[648,512]{1,0:T(8,128)(2,1)}) %reduce-scatter.8.cloned.1.call-update) | async-done | bytes 663568 | tf_op jit(solution)/shard_map/reduce_scatter | solution.py:180
  542.0 2.3 convert_add_fusion
  544.3 1.5 reshape.181
  545.8 1.8 copy.100
  (127 shorter events, 15.7 us)
Async XLA Ops:
  7.2 5.0 copy-start.25
  7.2 60.4 %all-gather.3.cloned.1.call-start = ((), (), s32[]{:S(2)}) async-start(), calls=%async_computation.3 | async-start | bytes 3317760 | tf_op jit(solution)/shard_map/all_gather | solution.py:118
  7.9 227.3 %reduce-scatter.6.cloned.1.call-start = ((), (), s32[]{:S(2)}) async-start(), calls=%async_computation.4 | async-start | bytes 3317760 | tf_op jit(solution)/shard_map/reduce_scatter | solution.py:133
  12.2 325.4 %copy-start.35 = (f32[128]{0:T(128)}, f32[128]{0:T(128)S(1)}, u32[]{:S(2)}) copy-start(f32[128]{0:T(128)S(1)} %get-tuple-element.175) | copy-start | bytes 1540
  12.2 325.4 %copy-start.37 = (f32[128]{0:T(128)}, f32[128]{0:T(128)S(1)}, u32[]{:S(2)}) copy-start(f32[128]{0:T(128)S(1)} %get-tuple-element.178) | copy-start | bytes 1540
  77.2 56.1 %copy-start.2 = (f32[648,128]{1,0:T(8,128)}, f32[648,128]{1,0:T(8,128)S(1)}, u32[]{:S(2)}) copy-start(f32[648,128]{1,0:T(8,128)S(1)} %get-tuple-element.180) | copy-start | bytes 995332
  150.0 2.5 copy-start.17
  150.0 2.6 copy-start.16
  150.0 2.6 copy-start.7
  151.3 1.4 copy-start.15
  152.5 1.1 copy-start.14
  152.6 1.2 copy-start.13
  152.7 1.5 copy-start.8
  154.0 2.6 copy-start.6
  156.5 29.3 %copy-start.10 = (f32[648,128]{1,0:T(8,128)}, f32[648,128]{1,0:T(8,128)S(1)}, u32[]{:S(2)}) copy-start(f32[648,128]{1,0:T(8,128)S(1)} %get-tuple-element.182) | copy-start | bytes 995332
  185.8 151.8 %all-gather.5.cloned.1.call-start = ((), (), s32[]{:S(2)}) async-start(), calls=%async_computation.5 | async-start | bytes 3317760 | tf_op jit(solution)/shard_map/all_gather | solution.py:146
  186.0 2.5 copy-start.22
  189.8 5.3 copy-start.24
  264.5 16.2 %copy-start.1 = (bf16[648,512]{1,0:T(8,128)(2,1)S(1)}, bf16[648,512]{1,0:T(8,128)(2,1)}, u32[]{:S(2)}) copy-start(bf16[648,512]{1,0:T(8,128)(2,1)} %reduce-scatter.6.cloned.1.call-done) | copy-start | bytes 1990660
  283.9 70.2 %copy-start.11 = (f32[648,128]{1,0:T(8,128)S(1)}, f32[648,128]{1,0:T(8,128)}, u32[]{:S(2)}) copy-start(f32[648,128]{1,0:T(8,128)} %copy-done.10) | copy-start | bytes 995332
  283.9 70.2 %copy-start.30 = (f32[128]{0:T(128)S(1)}, f32[128]{0:T(128)}, u32[]{:S(2)}) copy-start(f32[128]{0:T(128)} %get-tuple-element.150) | copy-start | bytes 1540
  284.0 126.4 %reduce-scatter.10.cloned.1.call-start = ((), (), s32[]{:S(2)}) async-start(), calls=%async_computation.7 | async-start | bytes 983040
  354.2 0.9 copy-start.31
  354.2 0.9 copy-start.33
  389.8 97.9 %all-reduce.17.cloned.1.call-start = ((), (), s32[]{:S(2)}) async-start(), calls=%async_computation.8 | async-start | bytes 4456448 | tf_op jit(solution)/shard_map/psum | solution.py:196
  389.8 9.3 %copy-start.12 = (f32[648,128]{1,0:T(8,128)S(1)}, f32[648,128]{1,0:T(8,128)}, u32[]{:S(2)}) copy-start(f32[648,128]{1,0:T(8,128)} %copy-done.10) | copy-start | bytes 995332
  389.9 9.3 %copy-start.36 = (f32[128]{0:T(128)S(1)}, f32[128]{0:T(128)}, u32[]{:S(2)}) copy-start(f32[128]{0:T(128)} %copy-done.35) | copy-start | bytes 1540
  389.9 9.3 %copy-start.38 = (f32[128]{0:T(128)S(1)}, f32[128]{0:T(128)}, u32[]{:S(2)}) copy-start(f32[128]{0:T(128)} %copy-done.37) | copy-start | bytes 1540
  402.5 9.0 %copy-start.3 = (f32[648,128]{1,0:T(8,128)S(1)}, f32[648,128]{1,0:T(8,128)}, u32[]{:S(2)}) copy-start(f32[648,128]{1,0:T(8,128)} %copy-done.2) | copy-start | bytes 995332
  402.5 21.7 %copy-start.29 = (f32[128]{0:T(128)S(1)}, f32[128]{0:T(128)}, u32[]{:S(2)}) copy-start(f32[128]{0:T(128)} %get-tuple-element.147) | copy-start | bytes 1540
  426.5 1.2 copy-start.5
  426.5 115.5 %reduce-scatter.8.cloned.1.call-start = ((), (), s32[]{:S(2)}) async-start(), calls=%async_computation.6 | async-start | bytes 3317760 | tf_op jit(solution)/shard_map/reduce_scatter | solution.py:180
  430.1 3.5 copy-start.26
  430.1 3.5 copy-start.27
  430.1 4.1 copy-start.34
  430.2 4.1 copy-start.32
  430.2 4.2 copy-start.28
  430.2 4.2 copy-start.39
  431.8 63.3 %slice-start = ((s8[4718592]{0:T(1024)(128)(4,1)}), s8[524288]{0:T(1024)(128)(4,1)S(1)}, s32[]{:S(2)}) async-start(s8[4718592]{0:T(1024)(128)(4,1)} %bitcast.121), calls=%async_computation.9 | async-start | bytes 1048576
  487.7 4.8 copy-start.9
  487.7 4.8 copy-start.19
  487.7 4.8 copy-start.21
  487.7 4.8 copy-start.23
  487.7 7.5 %slice-start.1 = ((s8[4718592]{0:T(1024)(128)(4,1)}), s8[4194304]{0:T(1024)(128)(4,1)S(1)}, s32[]{:S(2)}) async-start(s8[4718592]{0:T(1024)(128)(4,1)} %bitcast.121), calls=%async_computation.10 | async-start | bytes 8388608
  492.5 4.0 copy-start.4
  492.5 4.7 copy-start.18
  492.5 5.0 copy-start.20
  497.5 44.5 %copy-start = (f32[648,512]{1,0:T(8,128)S(1)}, f32[648,512]{1,0:T(8,128)}, u32[]{:S(2)}) copy-start(f32[648,512]{1,0:T(8,128)} %get-tuple-element.154) | copy-start | bytes 3981316
Sparse Core Ops, SparseCore 0:
  9.6 57.9 all-gather.2
  185.9 49.3 reduce-scatter.5
  284.1 53.4 all-gather.4
  389.9 20.3 reduce-scatter.9
  426.6 60.9 all-reduce.16
  489.9 52.0 reduce-scatter.7
where the time goes:
time: 556 us; the launch traced here: 555 us
  waiting for transfers between devices  244 us (44%)
  blocking collectives  130 us (23%)
  local copies, waits for them, and re-layouts  87.3 us (16%)
  other arithmetic  43 us (8%)
  matrix products  35.4 us (6%)
  between operations  14.7 us (3%)
    all_gather x1, waiting for transfers between devices, per_device(): piece = lax.all_gather(images, 'chan', axis=2, tiled=True)  55.5 us
    all_gather x1, waiting for transfers between devices, per_device(): third_full = lax.all_gather(third_low, 'chan', axis=1, tiled=True)  53.5 us
    psum x1, waiting for transfers between devices, per_device(): lax.psum(reduce_grad.astype(jnp.bfloat16), 'dp').astype(jnp.float32)  52.7 us
    reduce_scatter x1, waiting for transfers between devices, per_device(): lax.psum_scatter(partial_out.astype(jnp.bfloat16), 'chan', scatter_dimens...  40.1 us
    reduce_scatter x1, waiting for transfers between devices, per_device(): lax.psum_scatter(input_partial.astype(jnp.bfloat16), 'chan', scatter_dime...  39.8 us
    psum x3, blocking collectives, norm_forward(): lax.psum((jnp.sum(values * mask, axis=0), local_count), 'dp')  39.5 us
    psum x3, blocking collectives, norm_backward(): lax.psum((jnp.sum(incoming, axis=0), jnp.sum(incoming * normed, axis=0)),...  38 us
    psum x3, blocking collectives, norm_forward(): lax.psum(jnp.sum(mask * centered * centered, axis=0), 'dp') / count  35.4 us
  transfers between devices with their start and end apart: 6, of which 6 were waited for; matrix products, arithmetic and copies ran while one was open for 9% of the time, Pallas kernels for 0%

commit v1 on v0

v1 whole, which is shorter than its diff:
```python
import functools
import math

import jax
import jax.numpy as jnp
from jax import lax
from jax.experimental import pallas as pl
from jax.experimental.pallas import tpu as pltpu
from jax.sharding import PartitionSpec as P

MESH = pl.DeviceIdType.MESH
MAP = 9
PIX = MAP * MAP
TAPS = 9
PITCH = MAP + 1
STEP = 5
LANES = 128
CHUNK = 48

norm_eps = 1e-05
adam_eps = 1e-08
beta_one = 0.5
beta_two = 0.5
decay_rate = 0.05
ema_rate = 0.75
norm_rate = 0.3

F32 = jnp.float32
BF16 = jnp.bfloat16


def round_up(value, unit):
    return -(-value // unit) * unit


class Sizes:
    def __init__(self, mesh_dp, mesh_chan, images, reduce_weight):
        self.D, self.C = mesh_dp, mesh_chan
        self.Q = self.D // 2
        self.I, _, self.wp = images.shape
        self.ip, self.W = reduce_weight.shape
        self.K = self.ip * self.C
        self.KB = self.K // LANES
        self.WB = self.wp // LANES
        self.R = PIX * self.I
        self.RS = round_up(self.R, 16)
        self.RP = round_up(self.R, CHUNK)
        self.NW = self.WB * self.ip
        self.NS = TAPS * self.KB * self.ip
        self.PW = round_up(-(-self.NW // self.D), 16)
        self.PS = round_up(-(-self.NS // self.D), 16)
        self.PADROWS = ((MAP + 2) * PITCH + 2) * self.I


Z_PHASES = ["w2", "pre1", "act1", "par1", "act2", "par2", "grad2", "dlt2", "par3", "wsp", "zexp", "zred"]
D_PHASES = ["bn1", "bn2", "bn3", "bk3", "bk2", "bk1", "wdp"]
R_PHASES = [g + s for g in ("exp", "spa", "red") for s in ("core", "chip", "back", "pair")]
PHASES = Z_PHASES + D_PHASES + R_PHASES


def nt(a, b):
    return lax.dot_general(a, b, (((1,), (1,)), ((), ())), preferred_element_type=F32)


def nn(a, b):
    return lax.dot_general(a, b, (((1,), (0,)), ((), ())), preferred_element_type=F32)


def tn(a, b):
    return lax.dot_general(a, b, (((0,), (0,)), ((), ())), preferred_element_type=F32)


def sigmoid(v):
    return jax.nn.sigmoid(v)


def scratch_table(sz):
    C, D, Q, ip, wp, K, RP, I = sz.C, sz.D, sz.Q, sz.ip, sz.wp, sz.K, sz.RP, sz.I
    table = [
        ("xi", (I, PIX, wp), BF16),
        ("stage", (sz.WB, I * round_up(PIX, 8), LANES), F32),
        ("omap", (I, PIX, wp), F32),
        ("mask", (RP, LANES), F32),
        ("xb", (RP, wp), BF16),
        ("cotb", (RP, wp), BF16),
        ("w1f", (ip, sz.W), F32),
        ("w2f", (ip, sz.W), F32),
        ("w1s", (C, ip, wp), BF16),
        ("w1r", (C, ip, wp), BF16),
        ("w2s", (C, ip, wp), BF16),
        ("w2r", (C, ip, wp), BF16),
        ("wfull", (C, D * sz.PS, LANES), BF16),
        ("p1s", (C, RP, ip), BF16),
        ("p1r", (C, RP, ip), BF16),
        ("p2s", (C, RP, ip), BF16),
        ("p2r", (C, RP, ip), BF16),
        ("v1", (C, RP, ip), BF16),
        ("v2", (C, RP, ip), BF16),
        ("d2b", (C, RP, ip), BF16),
        ("pm1", (C, 8, ip), F32),
        ("pm2", (C, 8, ip), F32),
        ("pm3", (C, 8, ip), F32),
        ("st1", (D, 8, ip), F32),
        ("st2", (D, 8, ip), F32),
        ("st3", (D, 8, wp), F32),
        ("st4", (D, 8, wp), F32),
        ("st5", (D, 8, ip), F32),
        ("st6", (D, 8, K), F32),
        ("acc", (RP, ip), F32),
        ("pad", (sz.PADROWS, K), F32),
        ("cols", (TAPS, RP, K), BF16),
        ("act2", (RP, K), BF16),
        ("third", (RP, wp), F32),
        ("og", (RP, wp), F32),
        ("wide", (RP, wp), F32),
        ("tg", (RP, wp), BF16),
        ("big", (RP, K), F32),
        ("fag", (RP, K), F32),
        ("sgo", (RP, ip), BF16),
        ("fg", (RP, K), BF16),
    ]
    for name, z, part in (("exp", C, sz.PW), ("spa", 1, sz.PS), ("red", C, sz.PW)):
        table += [
            (name + "_gs", (2, Q, z, part, LANES), BF16),
            (name + "_rb", (Q, z, part, LANES), BF16),
            (name + "_sm", (Q, z, part, LANES), BF16),
            (name + "_rq", (Q, z, part, LANES), BF16),
            (name + "_tot", (z, part, LANES), BF16),
            (name + "_fin", (2, Q, z, part, LANES), BF16),
        ]
    return table


N_INPUTS, N_OUTPUTS = 8, 6


def block_kernel(sz, *refs):
    groups, images, cotangent, reduce_w, spatial_w, expand_w, inner_norm, outer_norm = refs[:8]
    out_hbm, ing_hbm, exp_hbm, spa_hbm, red_hbm, small_out = refs[8:14]
    table = scratch_table(sz)
    v = {name: ref for (name, _, _), ref in zip(table, refs[14:])}
    lsem, w1ssem, w1rsem, ssem, rsem = refs[14 + len(table) :]
    D, C, Q, I, K, KB, WB = sz.D, sz.C, sz.Q, sz.I, sz.K, sz.KB, sz.WB
    ip, wp, R, RS, RP = sz.ip, sz.wp, sz.R, sz.RS, sz.RP
    d = lax.axis_index("dp")
    c = lax.axis_index("chan")
    q = lax.div(d, 2)
    h = lax.rem(d, 2)
    zpeers = [lax.rem(c + k, C) for k in range(1, C)]
    dpeers = [lax.rem(d + k, D) for k in range(1, D)]
    qpeers = [lax.rem(q + k, Q) for k in range(1, Q)]
    sibling = d + 1 - 2 * h
    sem_of = {name: i for i, name in enumerate(PHASES)}
    sent = []

    def send(name, src, dst, device):
        pltpu.make_async_remote_copy(
            src_ref=src, dst_ref=dst, send_sem=ssem.at[sem_of[name]], recv_sem=rsem.at[sem_of[name]],
            device_id=device, device_id_type=MESH,
        ).start()

    def wait_bytes(ref, sem):
        pltpu.make_async_copy(ref, ref, sem).wait()

    def got(name, ref):
        wait_bytes(ref, rsem.at[sem_of[name]])
        sent.append((name, ref))

    barrier = pltpu.get_barrier_semaphore()
    for j in zpeers:
        pl.semaphore_signal(barrier, inc=1, device_id=(d, j), device_id_type=MESH)
    for e in dpeers:
        pl.semaphore_signal(barrier, inc=1, device_id=(e, c), device_id_type=MESH)

    xi, stage, omap, mask, xb, cotb = v["xi"], v["stage"], v["omap"], v["mask"], v["xb"], v["cotb"]
    w1f, w1s, w1r, w2f, w2s, w2r, wfull = (v[n] for n in ("w1f", "w1s", "w1r", "w2f", "w2s", "w2r", "wfull"))
    loads = [
        pltpu.make_async_copy(reduce_w, w1f, lsem.at[0]),
        pltpu.make_async_copy(images, xi, lsem.at[1]),
        pltpu.make_async_copy(expand_w, w2f, lsem.at[2]),
        pltpu.make_async_copy(spatial_w, wfull.at[c, pl.ds(0, sz.NS)], lsem.at[3]),
    ]
    for load in loads:
        load.start()

    def columns_of(ref, j):
        return ref[:, pl.ds(pl.multiple_of(j * wp, wp), wp)].astype(BF16)

    loads[0].wait()
    for j in zpeers:
        w1s[j] = columns_of(w1f, j)
    w1r[c] = columns_of(w1f, c)
    pl.semaphore_wait(barrier, C - 1 + D - 1)
    w1_copies = []
    for k, j in enumerate(zpeers):
        w1_copies.append(
            pltpu.make_async_remote_copy(
                src_ref=w1s.at[j], dst_ref=w1r.at[c], send_sem=w1ssem.at[k], recv_sem=w1rsem.at[k],
                device_id=(d, j), device_id_type=MESH,
            )
        )
        w1_copies[-1].start()

    row = lax.broadcasted_iota(jnp.int32, (I, LANES), 0)
    side = jnp.zeros((I, LANES), jnp.int32)
    for i in range(I):
        side = jnp.where(row == i, 5 + 2 * groups[i], side)
    cells_here = jnp.zeros((I, LANES), F32)
    for p in range(PIX):
        inside = (side > max(p // MAP, p % MAP)).astype(F32)
        mask[p * I : (p + 1) * I, :] = inside
        cells_here = cells_here + inside
    mask[R:RP, :] = jnp.zeros((RP - R, LANES), F32)
    count_here = jnp.sum(cells_here, axis=0, keepdims=True)
    img_rows = round_up(PIX, 8)

    def by_cell(src, dst):
        for i in range(I):
            values = src[i].astype(F32)
            for l in range(WB):
                stage[l, i * img_rows : i * img_rows + PIX, :] = values[:, l * LANES : (l + 1) * LANES]

        def pair(s, carry):
            for l in range(WB):
                both = [stage[l, pl.ds(2 * s + e, I, stride=img_rows), :] for e in range(2)]
                dst[pl.ds(pl.multiple_of(s * 2 * I, 2 * I), 2 * I), l * LANES : (l + 1) * LANES] = (
                    jnp.concatenate(both, axis=0).astype(BF16)
                )
            return carry

        lax.fori_loop(0, PIX // 2, pair, 0)
        for l in range(WB):
            last = stage[l, pl.ds(PIX - 1, I, stride=img_rows), :]
            rest = jnp.zeros((RP - R, LANES), F32)
            dst[R - I : RP, l * LANES : (l + 1) * LANES] = jnp.concatenate([last, rest], axis=0).astype(BF16)

    def by_image(src, dst):
        def cell(p, carry):
            for l in range(WB):
                stage[l, pl.ds(p, I, stride=img_rows), :] = src[
                    pl.ds(pl.multiple_of(p * I, I), I), l * LANES : (l + 1) * LANES
                ]
            return carry

        lax.fori_loop(0, PIX, cell, 0)
        for i in range(I):
            for l in range(WB):
                dst[i, :, l * LANES : (l + 1) * LANES] = stage[l, i * img_rows : i * img_rows + PIX, :]

    def lanes(values, width):
        if width <= LANES:
            return values[:, :width]
        return jnp.concatenate([values] * (width // LANES), axis=1)

    def mask_of(rows, width):
        return lanes(mask[rows, :], width)

    def over_chunks(body, carry=0):
        def step(s, carry):
            return body(pl.ds(pl.multiple_of(s * CHUNK, CHUNK), CHUNK), carry)

        return lax.fori_loop(0, RP // CHUNK, step, carry)

    def each_chunk(body):
        def step(rows, carry):
            body(rows)
            return carry

        over_chunks(step)

    def fold_rows(values):
        total = values[0:8]
        for s in range(1, values.shape[0] // 8):
            total = total + values[8 * s : 8 * s + 8]
        return total

    def total_of(values):
        return jnp.sum(values, axis=0, keepdims=True)

    def rows_of(*values):
        rest = jnp.zeros((8 - len(values), values[0].shape[1]), F32)
        return jnp.concatenate(list(values) + [rest], axis=0)

    loads[1].wait()
    by_cell(xi, xb)
    load_cot = pltpu.make_async_copy(cotangent, xi, lsem.at[4])
    load_cot.start()

    acc, p1s, p1r = v["acc"], v["p1s"], v["p1r"]
    for k in range(1, C):
        j = lax.rem(c - k + C, C)
        w1_copies[k - 1].wait_recv()
        p1s[j] = nt(xb[...], w1r[j]).astype(BF16)
        send("pre1", p1s.at[j, pl.ds(0, RS)], p1r.at[c, pl.ds(0, RS)], (d, j))
    acc[...] = nt(xb[...], w1r[c])
    loads[2].wait()
    for j in zpeers:
        w2s[j] = columns_of(w2f, j)
    w2r[c] = columns_of(w2f, c)
    for j in zpeers:
        send("w2", w2s.at[j], w2r.at[c], (d, j))
    load_cot.wait()
    by_cell(xi, cotb)
    loads[3].wait()

    def add_partials(name, recv):
        got(name, recv.at[pl.ds(0, C - 1), pl.ds(0, RS)])
        for j in zpeers:
            acc[0:RS, :] += recv[j, 0:RS, :].astype(F32)

    add_partials("pre1", p1r)

    def moments(src, width):
        def sums(rows, carry):
            return carry + fold_rows(src[rows, :] * mask_of(rows, width))

        mean = total_of(over_chunks(sums, jnp.zeros((8, width), F32))) / lanes(count_here, width)

        def squares(rows, carry):
            centered = src[rows, :] - mean
            return carry + fold_rows(mask_of(rows, width) * centered * centered)

        return mean, total_of(over_chunks(squares, jnp.zeros((8, width), F32)))

    def exchange_dp(name, table):
        for e in dpeers:
            send(name, table.at[d], table.at[d], (e, c))

    def combine(name, table):
        got(name, table.at[pl.ds(0, D - 1)])
        count = table[0, 2:3, :]
        average = count * table[0, 0:1, :]
        for e in range(1, D):
            count = count + table[e, 2:3, :]
            average = average + table[e, 2:3, :] * table[e, 0:1, :]
        average = average / count
        variance = jnp.zeros_like(average)
        for e in range(D):
            off = table[e, 0:1, :] - average
            variance = variance + (table[e, 1:2, :] + table[e, 2:3, :] * off * off)
        return average, lax.rsqrt(variance / count + norm_eps), count

    def sum_dp(name, table):
        got(name, table.at[pl.ds(0, D - 1)])
        total = table[0]
        for e in range(1, D):
            total = total + table[e]
        return total[0:1, :], total[1:2, :]

    def send_z(name, ref, rows=None):
        part = ref.at[c] if rows is None else ref.at[c, pl.ds(0, rows)]
        for j in zpeers:
            send(name, part, part, (d, j))

    def got_z(name, ref, rows=None):
        got(name, ref.at[pl.ds(0, C - 1)] if rows is None else ref.at[pl.ds(0, C - 1), pl.ds(0, rows)])

    def inner_forward(layer, bn, table, held, held_name, par, par_name):
        mean, spread = moments(acc, ip)
        table[d] = rows_of(mean, spread, lanes(count_here, ip))
        exchange_dp(bn, table)

        def center(rows):
            held[c, rows, :] = ((acc[rows, :] - mean) * mask_of(rows, ip)).astype(BF16)

        each_chunk(center)
        send_z(held_name, held, RS)
        average, inverse, count = combine(bn, table)
        par[c] = rows_of(
            inverse, (mean - average) * inverse,
            inner_norm[0, layer : layer + 1, :], inner_norm[1, layer : layer + 1, :],
        )
        send_z(par_name, par)
        got_z(held_name, held, RS)
        got_z(par_name, par)
        return count

    def joined(blocks, rows):
        return jnp.concatenate([blocks[j, rows, :].astype(F32) for j in range(C)], axis=1)

    def table_row(par, r):
        return jnp.concatenate([par[j, r : r + 1, :] for j in range(C)], axis=1)

    v1, v2, d2b, pm1, pm2, pm3 = (v[n] for n in ("v1", "v2", "d2b", "pm1", "pm2", "pm3"))
    for j in range(C):
        for ref in (v1, v2, d2b):
            ref[j, RS:RP, :] = jnp.zeros((RP - RS, ip), BF16)
    count_ip = inner_forward(0, "bn1", v["st1"], v1, "act1", pm1, "par1")

    def make_act(held, par, dst):
        inverse, shift, gain, bias = (table_row(par, r) for r in range(4))

        def step(rows):
            value = gain * (joined(held, rows) * inverse + shift) + bias
            dst[rows, :] = (value * sigmoid(value) * mask_of(rows, K)).astype(dst.dtype)

        each_chunk(step)

    big, pad, cols = v["big"], v["pad"], v["cols"]
    pad[...] = jnp.zeros_like(pad)
    make_act(v1, pm1, big)

    def fill_pad():
        for y in range(MAP):
            start = ((y + 1) * PITCH + 1) * I
            pad[start : start + MAP * I, :] = big[y * MAP * I : (y + 1) * MAP * I, :]

    def shifted(offset):
        pieces = [pad[pl.ds(pl.multiple_of(offset + y * PITCH * I, I), MAP * I), :] for y in range(MAP)]
        pieces.append(jnp.zeros((RP - R, K), F32))
        return jnp.concatenate(pieces, axis=0).astype(BF16)

    def weight_of(j, tap):
        pieces = [wfull[j, pl.ds(pl.multiple_of((tap * KB + kb) * ip, ip), ip), :] for kb in range(KB)]
        return jnp.concatenate(pieces, axis=1)

    fill_pad()
    acc[...] = jnp.zeros_like(acc)

    def second_step(tap, carry):
        cols[tap] = shifted((lax.div(tap, 3) * PITCH + lax.rem(tap, 3)) * I)
        acc[...] += nt(cols[tap], weight_of(c, tap))
        return carry

    lax.fori_loop(0, TAPS, second_step, 0)
    inner_forward(1, "bn2", v["st2"], v2, "act2", pm2, "par2")

    def part_of(j, e):
        return wfull.at[j, pl.ds(pl.multiple_of(e * sz.PS, 16), sz.PS)]

    for j in zpeers:
        send("wsp", part_of(c, d), part_of(c, d), (d, j))
    act2 = v["act2"]
    make_act(v2, pm2, act2)

    third, og, wide, tg = v["third"], v["og"], v["wide"], v["tg"]
    got_z("w2", w2r)
    third[...] = nn(act2[...], w2r[...].reshape(K, wp))
    mean3, spread3 = moments(third, wp)
    st3, st4, st5, st6 = v["st3"], v["st4"], v["st5"], v["st6"]
    st3[d] = rows_of(mean3, spread3, lanes(count_here, wp))
    exchange_dp("bn3", st3)
    average3, inverse3, count_wp = combine("bn3", st3)
    gain3, bias3 = outer_norm[0:1, :], outer_norm[1:2, :]

    def last_step(rows, carry):
        m = mask_of(rows, wp)
        normed = (third[rows, :] - average3) * inverse3
        third[rows, :] = normed
        summed = gain3 * normed + bias3 + xb[rows, :].astype(F32)
        s = sigmoid(summed)
        wide[rows, :] = summed * s * m
        grad = cotb[rows, :].astype(F32) * (s * (1.0 + summed * (1.0 - s))) * m
        og[rows, :] = grad
        return carry[0] + fold_rows(grad), carry[1] + fold_rows(grad * normed)

    zero_wp = jnp.zeros((8, wp), F32)
    sums = over_chunks(last_step, (zero_wp, zero_wp))
    st4[d] = rows_of(total_of(sums[0]), total_of(sums[1]))
    exchange_dp("bk3", st4)
    by_image(wide, omap)
    store_out = pltpu.make_async_copy(omap, out_hbm, lsem.at[5])
    store_out.start()
    bias_grad3, gain_grad3 = sum_dp("bk3", st4)
    scale3 = inverse3 * gain3

    def third_step(rows):
        back = mask_of(rows, wp) * ((bias_grad3 + third[rows, :] * gain_grad3) / count_wp)
        tg[rows, :] = (scale3 * (og[rows, :] - back)).astype(BF16)

    each_chunk(third_step)

    p2s, p2r = v["p2s"], v["p2r"]
    for k in range(1, C):
        j = lax.rem(c - k + C, C)
        p2s[j] = nt(tg[...], w2r[j]).astype(BF16)
        send("grad2", p2s.at[j, pl.ds(0, RS)], p2r.at[c, pl.ds(0, RS)], (d, j))
    acc[...] = nt(tg[...], w2r[c])

    class Reduction:
        def __init__(self, name, z, part):
            self.name, self.z, self.part = name, z, part
            self.gs, self.rb, self.sm, self.rq, self.tot, self.fin = (
                v[name + "_" + s] for s in ("gs", "rb", "sm", "rq", "tot", "fin")
            )

        def put(self, zi, block, value):
            row, end = block * ip, (block + 1) * ip
            while row < end:
                owner = row // self.part
                stop = min(end, (owner + 1) * self.part)
                at = row - owner * self.part
                self.gs[owner % 2, owner // 2, zi, at : at + stop - row, :] = value[
                    row - block * ip : stop - block * ip, :
                ]
                row = stop

        def pair(self):
            send(self.name + "core", self.gs.at[1 - h], self.rb, (sibling, c))

        def chips(self):
            got(self.name + "core", self.rb)
            for e in range(Q):
                self.sm[e] = (self.gs[h, e].astype(F32) + self.rb[e].astype(F32)).astype(BF16)
            for e in qpeers:
                send(self.name + "chip", self.sm.at[e], self.rq.at[q], (2 * e + h, c))

        def chan(self):
            got(self.name + "chip", self.rq.at[pl.ds(0, Q - 1)])
            total = self.sm[q].astype(F32)
            for e in qpeers:
                total = total + self.rq[e].astype(F32)
            self.tot[...] = total.astype(BF16)
            if self.z == 1:
                self.fin[h, q, 0] = self.tot[0]
            else:
                self.fin[h, q, c] = self.tot[c]
                for j in zpeers:
                    send("z" + self.name, self.tot.at[j], self.fin.at[h, q, c], (d, j))

        def back(self):
            if self.z > 1:
                got("z" + self.name, self.fin.at[h, q, pl.ds(0, C - 1)])
            for e in qpeers:
                send(self.name + "back", self.fin.at[h, q], self.fin.at[h, q], (2 * e + h, c))

        def other(self):
            got(self.name + "back", self.fin.at[h, pl.ds(0, Q - 1)])
            send(self.name + "pair", self.fin.at[h], self.fin.at[h], (sibling, c))

        def done(self):
            got(self.name + "pair", self.fin.at[0])

    exp_red = Reduction("exp", C, sz.PW)
    spa_red = Reduction("spa", 1, sz.PS)
    red_red = Reduction("red", C, sz.PW)
    for j in range(C):
        block = tn(act2[:, j * ip : (j + 1) * ip], tg[...]).astype(BF16)
        for wb in range(WB):
            exp_red.put(j, wb, block[:, wb * LANES : (wb + 1) * LANES])
    exp_red.pair()

    add_partials("grad2", p2r)
    inverse_own, shift_own, gain_own, bias_own = (pm2[c, r : r + 1, :] for r in range(4))

    def second_back(rows, carry):
        normed = v2[c, rows, :].astype(F32) * inverse_own + shift_own
        value = gain_own * normed + bias_own
        s = sigmoid(value)
        grad = acc[rows, :] * (s * (1.0 + value * (1.0 - s))) * mask_of(rows, ip)
        d2b[c, rows, :] = grad.astype(BF16)
        return carry[0] + fold_rows(grad), carry[1] + fold_rows(grad * normed)

    zero_ip = jnp.zeros((8, ip), F32)
    sums = over_chunks(second_back, (zero_ip, zero_ip))
    st5[d] = rows_of(total_of(sums[0]), total_of(sums[1]))
    exchange_dp("bk2", st5)
    send_z("dlt2", d2b, RS)
    exp_red.chips()
    got("wsp", wfull.at[pl.ds(0, C - 1), pl.ds(0, sz.PS)])
    for j in zpeers:
        for e in dpeers:
            send("wdp", part_of(j, d), part_of(j, d), (e, c))
    bias_grad2, gain_grad2 = sum_dp("bk2", st5)
    pm3[c] = rows_of(bias_grad2 / count_ip, gain_grad2 / count_ip)
    send_z("par3", pm3)
    sgo = v["sgo"]

    def own_second(rows):
        normed = v2[c, rows, :].astype(F32) * inverse_own + shift_own
        back = mask_of(rows, ip) * (pm3[c, 0:1, :] + normed * pm3[c, 1:2, :])
        sgo[rows, :] = (inverse_own * gain_own * (d2b[c, rows, :].astype(F32) - back)).astype(BF16)

    each_chunk(own_second)
    for tap in range(TAPS):
        block = tn(sgo[...], cols[tap]).astype(BF16)
        for kb in range(KB):
            spa_red.put(0, tap * KB + kb, block[:, kb * LANES : (kb + 1) * LANES])
    exp_red.chan()
    spa_red.pair()
    got_z("dlt2", d2b, RS)
    got_z("par3", pm3)
    inverse2, shift2, gain2 = (table_row(pm2, r) for r in range(3))
    bias_part, gain_part = table_row(pm3, 0), table_row(pm3, 1)
    scale2 = inverse2 * gain2

    def full_second(rows):
        normed = joined(v2, rows) * inverse2 + shift2
        back = mask_of(rows, K) * (bias_part + normed * gain_part)
        big[rows, :] = (scale2 * (joined(d2b, rows) - back)).astype(BF16).astype(F32)

    each_chunk(full_second)
    fill_pad()
    spa_red.chips()
    exp_red.back()
    got("wdp", wfull.at[pl.ds(0, C - 1), pl.ds(0, (D - 1) * sz.PS)])

    fag = v["fag"]
    fag[...] = jnp.zeros_like(fag)

    def first_act_step(tap, carry):
        offset = ((2 - lax.div(tap, 3)) * PITCH + 2 - lax.rem(tap, 3)) * I
        weight = jnp.concatenate([weight_of(j, tap) for j in range(C)], axis=0)
        fag[...] += nn(shifted(offset), weight)
        return carry

    lax.fori_loop(0, TAPS, first_act_step, 0)
    inverse1, shift1, gain1, bias1 = (table_row(pm1, r) for r in range(4))

    def first_back(rows, carry):
        normed = joined(v1, rows) * inverse1 + shift1
        value = gain1 * normed + bias1
        s = sigmoid(value)
        grad = fag[rows, :] * (s * (1.0 + value * (1.0 - s))) * mask_of(rows, K)
        fag[rows, :] = grad
        big[rows, :] = normed
        return carry[0] + fold_rows(grad), carry[1] + fold_rows(grad * normed)

    zero_k = jnp.zeros((8, K), F32)
    sums = over_chunks(first_back, (zero_k, zero_k))
    st6[d] = rows_of(total_of(sums[0]), total_of(sums[1]))
    exchange_dp("bk1", st6)
    spa_red.chan()
    spa_red.back()
    exp_red.other()
    bias_grad1, gain_grad1 = sum_dp("bk1", st6)
    scale1 = inverse1 * gain1
    count_k = lanes(count_ip[:, 0:1] + jnp.zeros((1, LANES), F32), K)
    fg = v["fg"]

    def first_step(rows):
        back = mask_of(rows, K) * ((bias_grad1 + big[rows, :] * gain_grad1) / count_k)
        fg[rows, :] = (scale1 * (fag[rows, :] - back)).astype(BF16)

    each_chunk(first_step)
    for j in range(C):
        block = tn(fg[:, j * ip : (j + 1) * ip], xb[...]).astype(BF16)
        for wb in range(WB):
            red_red.put(j, wb, block[:, wb * LANES : (wb + 1) * LANES])
    red_red.pair()
    wide[...] = nn(fg[...], w1r[...].reshape(K, wp)) + og[...]
    red_red.chips()
    spa_red.other()
    exp_red.done()
    store_out.wait()
    by_image(wide, omap)
    store_in = pltpu.make_async_copy(omap, ing_hbm, lsem.at[6])
    store_in.start()
    red_red.chan()
    red_red.back()
    store_exp = pltpu.make_async_copy(exp_red.fin, exp_hbm, lsem.at[7])
    store_exp.start()
    spa_red.done()
    store_spa = pltpu.make_async_copy(spa_red.fin, spa_hbm, lsem.at[8])
    store_spa.start()
    small_out[...] = jnp.zeros_like(small_out)
    small_out[0:1, 0:K] = gain_grad1
    small_out[1:2, 0:K] = bias_grad1
    small_out[2:3, 0:ip] = gain_grad2
    small_out[3:4, 0:ip] = bias_grad2
    small_out[4:5, 0:wp] = gain_grad3
    small_out[5:6, 0:wp] = bias_grad3
    red_red.other()
    red_red.done()
    store_red = pltpu.make_async_copy(red_red.fin, red_hbm, lsem.at[9])
    store_red.start()
    for copy in (store_in, store_exp, store_spa, store_red):
        copy.wait()
    for copy in w1_copies:
        copy.wait_send()
    for name, ref in sent:
        wait_bytes(ref, ssem.at[sem_of[name]])


def adamw(weight, moments, average, grad, rate, decay):
    first = beta_one * moments[0] + (1.0 - beta_one) * grad
    second = beta_two * moments[1] + (1.0 - beta_two) * grad * grad
    corr_one = 1.0 - beta_one**STEP
    corr_two = 1.0 - beta_two**STEP
    new_weight = weight - rate * (
        first / corr_one / (jnp.sqrt(second / corr_two) + adam_eps) + decay * weight
    )
    new_average = ema_rate * average + (1.0 - ema_rate) * new_weight
    return (new_weight, first, second, new_average)


def per_device(
    mesh_dp, mesh_chan,
    images, groups, cotangent, reduce_weight, spatial_weight, expand_weight, inner_norm, outer_norm,
    reduce_moments, spatial_moments, expand_moments, inner_moments, outer_moments,
    reduce_ema, spatial_ema, expand_ema, inner_ema, outer_ema,
):
    sz = Sizes(mesh_dp, mesh_chan, images, reduce_weight)
    ip, K, D = sz.ip, sz.K, sz.D
    spatial_low = (
        spatial_weight.reshape(ip, TAPS * sz.KB, LANES).transpose(1, 0, 2).reshape(sz.NS, LANES).astype(BF16)
    )
    wide_row = max(K, sz.wp)
    any_spec, vmem_spec = pl.BlockSpec(memory_space=pl.ANY), pl.BlockSpec(memory_space=pltpu.VMEM)
    output, input_grad, exp_sum, spa_sum, red_sum, small = pl.pallas_call(
        functools.partial(block_kernel, sz),
        out_shape=(
            jax.ShapeDtypeStruct(images.shape, F32),
            jax.ShapeDtypeStruct(images.shape, F32),
            jax.ShapeDtypeStruct((2, sz.Q, sz.C, sz.PW, LANES), BF16),
            jax.ShapeDtypeStruct((2, sz.Q, 1, sz.PS, LANES), BF16),
            jax.ShapeDtypeStruct((2, sz.Q, sz.C, sz.PW, LANES), BF16),
            jax.ShapeDtypeStruct((8, wide_row), F32),
        ),
        in_specs=[pl.BlockSpec(memory_space=pltpu.SMEM)] + [any_spec] * 5 + [vmem_spec] * 2,
        out_specs=(any_spec,) * 5 + (vmem_spec,),
        scratch_shapes=[pltpu.VMEM(shape, dtype) for _, shape, dtype in scratch_table(sz)]
        + [
            pltpu.SemaphoreType.DMA((10,)),
            pltpu.SemaphoreType.DMA((sz.C - 1,)),
            pltpu.SemaphoreType.DMA((sz.C - 1,)),
            pltpu.SemaphoreType.DMA((len(PHASES),)),
            pltpu.SemaphoreType.DMA((len(PHASES),)),
        ],
        compiler_params=pltpu.CompilerParams(
            collective_id=0, has_side_effects=True, vmem_limit_bytes=60 * 2**20
        ),
    )(groups, images, cotangent, reduce_weight, spatial_low, expand_weight, inner_norm, outer_norm)

    def whole(parts, z, n, cols):
        rows = parts.transpose(2, 1, 0, 3, 4).reshape(z, -1, LANES)[:, :n]
        rows = rows.reshape(z * n // ip, ip, LANES).transpose(1, 0, 2)
        return rows.reshape(ip, cols).astype(F32)

    exp_grad = whole(exp_sum, sz.C, sz.NW, sz.W)
    red_grad = whole(red_sum, sz.C, sz.NW, sz.W)
    spa_grad = whole(spa_sum, 1, sz.NS, TAPS * K).reshape(spatial_weight.shape)
    own = lax.axis_index("chan") * ip
    first_rows = lax.dynamic_slice(small[0:2, :K], (0, own), (2, ip))
    inner_grad = jnp.stack(
        [jnp.stack([first_rows[0], small[2, :ip]]), jnp.stack([first_rows[1], small[3, :ip]])]
    )
    outer_grad = small[4:6, : sz.wp]
    new_reduce = adamw(reduce_weight, reduce_moments, reduce_ema, red_grad, 2.0 / math.sqrt(sz.W), decay_rate)
    new_spatial = adamw(
        spatial_weight, spatial_moments, spatial_ema, spa_grad, 2.0 / math.sqrt(TAPS * K), decay_rate
    )
    new_expand = adamw(expand_weight, expand_moments, expand_ema, exp_grad, 2.0 / math.sqrt(K), decay_rate)
    new_inner = adamw(inner_norm, inner_moments, inner_ema, inner_grad, norm_rate, 0.0)
    new_outer = adamw(outer_norm, outer_moments, outer_ema, outer_grad, norm_rate, 0.0)
    return (output, input_grad, *new_reduce, *new_spatial, *new_expand, *new_inner, *new_outer)


def solution(mesh):
    placed = (
        P("dp", None, "chan"),
        P("dp"),
        P("dp", None, "chan"),
        P("chan", None),
        P("chan", None, None, None),
        P("chan", None),
        P(None, None, "chan"),
        P(None, "chan"),
        P(None, "chan", None),
        P(None, "chan", None, None, None),
        P(None, "chan", None),
        P(None, None, None, "chan"),
        P(None, None, "chan"),
        P("chan", None),
        P("chan", None, None, None),
        P("chan", None),
        P(None, None, "chan"),
        P(None, "chan"),
    )
    return jax.shard_map(
        functools.partial(per_device, mesh.shape["dp"], mesh.shape["chan"]),
        mesh=mesh,
        in_specs=placed,
        out_specs=(P("dp", None, "chan"),) * 2
        + (P("chan", None),) * 4
        + (P("chan", None, None, None),) * 4
        + (P("chan", None),) * 4
        + (P(None, None, "chan"),) * 4
        + (P(None, "chan"),) * 4,
        check_vma=False,
    )
```

time: 556 us -> 301 us (0.54)
  waiting for transfers between devices: 244 us -> 0 us
  Pallas kernels: 0 us -> 188 us
  blocking collectives: 130 us -> 0 us
  matrix products: 35.4 us -> 0 us
  other arithmetic: 43 us -> 22.7 us
  between operations: 14.7 us -> 0.83 us
    pallas_call x0 -> x1, Pallas kernels: none -> 188 us  [per_device(): pl.pallas_call(functools.partial(block_kernel, sz), out_shape=(jax.ShapeD...]
    psum x9 -> x0, blocking collectives: 113 us -> none  [the longest x3 39.5 us: norm_forward(): lax.psum((jnp.sum(values * mask, axis=0), local_count), 'dp')]
    all_gather x2 -> x0, waiting for transfers between devices: 109 us -> none  [the longest x1 55.5 us: per_device(): piece = lax.all_gather(images, 'chan', axis=2, tiled=True)]
    reduce_scatter x2 -> x0, waiting for transfers between devices: 80 us -> none  [the longest x1 40.1 us: per_device(): lax.psum_scatter(partial_out.astype(jnp.bfloat16), 'chan', scatter_dimens...]
    psum x1 -> x0, waiting for transfers between devices: 52.7 us -> none  [per_device(): lax.psum(reduce_grad.astype(jnp.bfloat16), 'dp').astype(jnp.float32)]
    unnamed x97 -> x56, local copies, waits for them, and re-layouts: 16.8 us -> 64.7 us
    dot_general x9 -> x0, matrix products: 35.4 us -> none  [the longest x1 11.3 us: per_device(): jnp.einsum('rk,kt->rt', second_low, spatial_low, preferred_element_type=j...]
    all_gather x1 -> x0, blocking collectives: 17.1 us -> none  [per_device(): first_full = lax.all_gather(first_act, 'chan', axis=1, tiled=True)]
  transfers between devices with their start and end apart: 6 -> 0, of which waited for: 6 -> 0; matrix products, arithmetic and copies ran while one was open for 9% -> 0% of each run, Pallas kernels for 0% -> 0%
where the time goes in v1:
time: 301 us; the launch traced here: 300 us
  Pallas kernels  188 us (62%)
  local copies, waits for them, and re-layouts  88.3 us (29%)
  other arithmetic  22.7 us (8%)
    pallas_call x1, Pallas kernels, per_device(): pl.pallas_call(functools.partial(block_kernel, sz), out_shape=(jax.ShapeD...  188 us
    unnamed x56, local copies, waits for them, and re-layouts  64.7 us
    add x5, other arithmetic, adamw(): new_average = ema_rate * average + (1.0 - ema_rate) * new_weight  19.7 us
    slice x3, local copies, waits for them, and re-layouts, adamw(): second = beta_two * moments[1] + (1.0 - beta_two) * grad * grad  11.4 us
    convert_element_type x6, local copies, waits for them, and re-layouts, whole(): return rows.reshape(ip, cols).astype(F32)  10.8 us

profile of v1, /device:TPU:0, one launch (start us, length us, event | category | flops | bytes accessed | tf_op | source)
XLA Modules:
  0.0 299.6 jit_solution(8659457428032740963)
XLA Ops:
  0.7 2.1 copy.65.refs_1_
  2.8 2.1 copy.66.refs_2_
  4.9 2.0 copy.63
  7.0 0.2 convert_element_type.55
  7.2 1.4 copy.64
  8.6 187.7 %shard_map.345 = (f32[8,81,512]{2,1,0:T(8,128)}, f32[8,81,512]{2,1,0:T(8,128)}, bf16[2,4,4,64,128]{4,3,2,1,0:T(8,128)(2,1)}, bf16[2,4,1,576,128]{4,3,2,1,0:T(8,1...) custom-call(s32[8]{0:T(128)} %refs_0_.1, bf16[8,81,512]{2,1,0:T(8,128)(2,1)} %copy.65.refs_1_, ...), custom_call_target="tpu_custom_call" | custom-call | tf_op jit(solution)/shard_map/pallas_call | solution.py:700
  196.3 0.0 copy-start.6
  196.3 3.3 %copy.88 = f32[8,81,512]{2,0,1:T(8,128)} copy(f32[8,81,512]{2,1,0:T(8,128)} %get-tuple-element.78) | data formatting | bytes 2654208
  199.6 0.0 copy-done.6
  199.6 1.8 copy.89
  201.5 2.5 copy.73
  204.0 0.0 copy-done.5
  204.0 1.3 copy.72
  205.3 1.4 convert_bitcast_fusion.1
  206.8 1.0 copy.68
  207.8 2.5 copy.69
  210.3 3.1 %fusion.12 = (f32[1,128,2048]{2,1,0:T(8,128)}, f32[1,128,2048]{2,1,0:T(8,128)}) fusion(f32[2,128,2048]{2,1,0:T(8,128)} %param.26), kind=kLoop, calls=%fused_computation.34 | loop fusion | bytes 4194304 | tf_op jit(solution)/shard_map/slice | solution.py:677
  213.4 2.5 copy.102
  215.9 2.5 copy.103
  218.5 5.1 %multiply_add_fusion.5 = (f32[128,2048]{0,1:T(8,128)}, f32[128,2048]{0,1:T(8,128)}, f32[128,2048]{0,1:T(8,128)}, f32[128,2048]{0,1:T(8,128)}) fusion(f32[128,2048]{0,1:T(8,128)} %copy.73, f32[128,2048]{0,1:T(8,128)} %copy.72, f32[128,16,128]{0,2,1:T(8,128)} %copy.69, f32[1,128,2048]{1,2,0:T(8,128)} %copy.102, f32[1,128,2048]{1,2,0:T(8,128)} %copy.103), kind=kLoop, calls=%fused_computation.16 | loop fusion | flops 4456448 | bytes 9437184 | tf_op jit(solution)/shard_map/add | solution.py:683
  223.6 2.5 copy.90
  226.2 2.5 copy.91
  228.7 2.5 copy.92
  231.2 2.5 copy.93
  233.7 3.0 %copy.80 = f32[128,3,3,512]{0,3,2,1:T(8,128)} copy(f32[128,3,3,512]{3,0,2,1:T(8,128)} %param.32) | data formatting | bytes 4718592 | tf_op args[14]
  236.8 1.4 convert_bitcast_fusion
  238.2 1.6 copy.75
  239.8 3.0 %copy.76 = f32[128,36,128]{0,2,1:T(8,128)} copy(f32[128,36,128]{2,0,1:T(8,128)} %bitcast.64) | data formatting | bytes 4718592 | tf_op jit(solution)/shard_map/convert_element_type | solution.py:728
  242.8 5.3 %fusion.10 = (f32[1,128,3,3,512]{4,1,3,2,0:T(8,128)}, f32[1,128,3,3,512]{4,1,3,2,0:T(8,128)}) fusion(f32[2,128,3,3,512]{4,1,3,2,0:T(8,128)} %param.27), kind=kLoop, calls=%fused_computation.32 | loop fusion | bytes 9437184 | tf_op jit(solution)/shard_map/slice | solution.py:677
  248.1 3.1 %copy.104 = f32[1,128,3,3,512]{1,4,3,2,0:T(8,128)} copy(f32[1,128,3,3,512]{4,1,3,2,0:T(8,128)} %get-tuple-element.121) | data formatting | bytes 4718592
  251.1 3.0 %copy.105 = f32[1,128,3,3,512]{1,4,3,2,0:T(8,128)} copy(f32[1,128,3,3,512]{4,1,3,2,0:T(8,128)} %get-tuple-element.120) | data formatting | bytes 4718592
  254.2 9.0 %multiply_add_fusion.1 = (f32[128,3,3,512]{0,3,2,1:T(8,128)}, f32[128,3,3,512]{0,3,2,1:T(8,128)}, f32[128,3,3,512]{0,3,2,1:T(8,128)}, f32[128,3,3,512]{0,3,2,1:T(8,128)}) fusion(f32[128,3,3,512]{0,3,2,1:T(8,128)} %copy.80, f32[128,3,3,512]{0,3,2,1:T(8,128)S(1)} %copy.63, f32[128,3,3,512]{0,3,2,1:T(8,128)} %bitcast.65, f32[1,128,3,3,512]{1,4,3,2,0:T(8,128)} %copy.104, ...), kind=kLoop, calls=%fused_computation.4 | loop fusion | flops 10027008 | bytes 21233664 | tf_op jit(solution)/shard_map/add | solution.py:683
  263.2 3.2 %copy.94 = f32[128,3,3,512]{3,0,2,1:T(8,128)} copy(f32[128,3,3,512]{0,3,2,1:T(8,128)} %get-tuple-element.113) | data formatting | bytes 4718592
  266.4 0.0 copy-done.1
  266.4 1.9 copy.95
  268.3 3.2 %copy.96 = f32[128,3,3,512]{3,0,2,1:T(8,128)} copy(f32[128,3,3,512]{0,3,2,1:T(8,128)} %get-tuple-element.115) | data formatting | bytes 4718592
  271.5 0.0 copy-done
  271.5 1.9 copy.97
  273.5 1.5 copy.87
  275.0 1.6 copy.86
  276.6 1.0 copy.82
  277.6 1.6 copy.83
  279.2 3.1 %fusion.11 = (f32[1,128,2048]{2,1,0:T(8,128)}, f32[1,128,2048]{2,1,0:T(8,128)}) fusion(f32[2,128,2048]{2,1,0:T(8,128)} %param.28), kind=kLoop, calls=%fused_computation.33 | loop fusion | bytes 4194304 | tf_op jit(solution)/shard_map/slice | solution.py:677
  282.3 2.5 copy.106
  284.8 2.5 copy.107
  287.3 4.3 %multiply_add_fusion.4 = (f32[128,2048]{0,1:T(8,128)}, f32[128,2048]{0,1:T(8,128)}, f32[128,2048]{0,1:T(8,128)}, f32[128,2048]{0,1:T(8,128)}) fusion(f32[128,2048]{0,1:T(8,128)S(1)} %copy.87, f32[128,2048]{0,1:T(8,128)S(1)} %copy.86, f32[128,16,128]{0,2,1:T(8,128)S(1)} %copy.83, f32[1,128,2048]{1,2,0:T(8,128)} %copy.106, f32[1,128,2048]{1,2,0:T(8,128)} %copy.107), kind=kLoop, calls=%fused_computation.14 | loop fusion | flops 4456448 | bytes 9437184 | tf_op jit(solution)/shard_map/add | solution.py:683
  291.7 2.7 copy.98
  294.3 0.0 copy-done.4
  294.3 1.3 copy.99
  295.7 0.0 copy-start.8
  295.7 0.0 copy-start.11
  295.7 0.0 copy-start.13
  295.7 0.0 copy-done.3
  295.7 1.3 copy.100
  297.0 0.0 copy-done.2
  297.0 1.3 copy.101
  298.3 0.0 copy-done.10
  298.3 0.0 copy-done.7
  298.3 0.0 copy-done.9
  298.3 0.0 copy-done.12
  298.4 0.6 multiply_add_fusion.7
  299.0 0.0 copy-done.8
  299.0 0.0 copy-done.11
  299.0 0.6 multiply_add_fusion.9
  (15 shorter events, 0.0 us)
Async XLA Ops:
  196.3 3.3 %copy-start.6 = (f32[8,81,512]{2,1,0:T(8,128)S(1)}, f32[8,81,512]{2,1,0:T(8,128)}, u32[]{:S(2)}) copy-start(f32[8,81,512]{2,1,0:T(8,128)} %get-tuple-element.79) | copy-start | bytes 3981316
  199.6 4.4 %copy-start.5 = (f32[128,2048]{1,0:T(8,128)S(1)}, f32[128,2048]{1,0:T(8,128)}, u32[]{:S(2)}) copy-start(f32[128,2048]{1,0:T(8,128)} %refs_3_.1) | copy-start | bytes 3145732
  263.2 3.2 %copy-start.1 = (f32[128,3,3,512]{0,3,2,1:T(8,128)S(1)}, f32[128,3,3,512]{0,3,2,1:T(8,128)}, u32[]{:S(2)}) copy-start(f32[128,3,3,512]{0,3,2,1:T(8,128)} %get-tuple-element.114) | copy-start | bytes 7077892
  268.3 3.2 %copy-start = (f32[128,3,3,512]{0,3,2,1:T(8,128)S(1)}, f32[128,3,3,512]{0,3,2,1:T(8,128)}, u32[]{:S(2)}) copy-start(f32[128,3,3,512]{0,3,2,1:T(8,128)} %get-tuple-element.112) | copy-start | bytes 7077892
  291.7 2.7 copy-start.4
  291.7 4.0 %copy-start.3 = (f32[128,2048]{0,1:T(8,128)S(1)}, f32[128,2048]{0,1:T(8,128)}, u32[]{:S(2)}) copy-start(f32[128,2048]{0,1:T(8,128)} %get-tuple-element.111) | copy-start | bytes 3145732
  294.3 2.7 copy-start.2
  295.6 2.7 copy-start.10
  295.7 2.7 copy-start.7
  295.7 2.7 copy-start.9
  295.7 2.7 copy-start.12
  295.7 3.3 %copy-start.8 = (f32[2,2,128]{2,1,0:T(2,128)S(1)}, f32[2,2,128]{2,1,0:T(2,128)}, u32[]{:S(2)}) copy-start(f32[2,2,128]{2,1,0:T(2,128)} %refs_6_.1) | copy-start | bytes 6148
  295.7 3.3 %copy-start.11 = (f32[2,2,2,128]{3,2,1,0:T(2,128)S(1)}, f32[2,2,2,128]{3,2,1,0:T(2,128)}, u32[]{:S(2)}) copy-start(f32[2,2,2,128]{3,2,1,0:T(2,128)} %param.29) | copy-start | bytes 12292
  295.7 3.3 %copy-start.13 = (f32[2,2,128]{2,1,0:T(2,128)S(1)}, f32[2,2,128]{2,1,0:T(2,128)}, u32[]{:S(2)}) copy-start(f32[2,2,128]{2,1,0:T(2,128)} %param.34) | copy-start | bytes 6148

commit v2 on v1

--- a/solution.py
+++ b/solution.py
@@ -16,6 +16,7 @@
 STEP = 5
 LANES = 128
 CHUNK = 48
+VMEM_TOTAL = 62 * 2**20
 
 norm_eps = 1e-05
 adam_eps = 1e-08
@@ -45,9 +46,8 @@
         self.R = PIX * self.I
         self.RS = round_up(self.R, 16)
         self.RP = round_up(self.R, CHUNK)
-        self.NW = self.WB * self.ip
-        self.NS = TAPS * self.KB * self.ip
-        self.PW = round_up(-(-self.NW // self.D), 16)
+        self.NS = TAPS * self.ip
+        self.PW = round_up(-(-self.ip // self.D), 16)
         self.PS = round_up(-(-self.NS // self.D), 16)
         self.PADROWS = ((MAP + 2) * PITCH + 2) * self.I
 
@@ -74,25 +74,26 @@
     return jax.nn.sigmoid(v)
 
 
+def vmem_bytes(shape, dtype):
+    *lead, rows, width = shape
+    return math.prod(lead) * round_up(rows, 8) * round_up(width, LANES) * jnp.dtype(dtype).itemsize
+
+
 def scratch_table(sz):
     C, D, Q, ip, wp, K, RP, I = sz.C, sz.D, sz.Q, sz.ip, sz.wp, sz.K, sz.RP, sz.I
     table = [
-        ("xi", (I, PIX, wp), BF16),
-        ("stage", (sz.WB, I * round_up(PIX, 8), LANES), F32),
-        ("omap", (I, PIX, wp), F32),
+        ("xi", (sz.R, wp), BF16),
+        ("coti", (sz.R, wp), BF16),
         ("mask", (RP, LANES), F32),
         ("xb", (RP, wp), BF16),
         ("cotb", (RP, wp), BF16),
-        ("w1f", (ip, sz.W), F32),
-        ("w2f", (ip, sz.W), F32),
         ("w1s", (C, ip, wp), BF16),
         ("w1r", (C, ip, wp), BF16),
         ("w2s", (C, ip, wp), BF16),
         ("w2r", (C, ip, wp), BF16),
-        ("wfull", (C, D * sz.PS, LANES), BF16),
+        ("wfull", (C, D * sz.PS, K), BF16),
         ("p1s", (C, RP, ip), BF16),
         ("p1r", (C, RP, ip), BF16),
-        ("p2s", (C, RP, ip), BF16),
         ("p2r", (C, RP, ip), BF16),
         ("v1", (C, RP, ip), BF16),
         ("v2", (C, RP, ip), BF16),
@@ -100,6 +101,7 @@
         ("pm1", (C, 8, ip), F32),
         ("pm2", (C, 8, ip), F32),
         ("pm3", (C, 8, ip), F32),
+        ("own", (C, 8, ip), F32),
         ("st1", (D, 8, ip), F32),
         ("st2", (D, 8, ip), F32),
         ("st3", (D, 8, wp), F32),
@@ -112,34 +114,31 @@
         ("act2", (RP, K), BF16),
         ("third", (RP, wp), F32),
         ("og", (RP, wp), F32),
-        ("wide", (RP, wp), F32),
         ("tg", (RP, wp), BF16),
         ("big", (RP, K), F32),
         ("fag", (RP, K), F32),
         ("sgo", (RP, ip), BF16),
         ("fg", (RP, K), BF16),
     ]
-    for name, z, part in (("exp", C, sz.PW), ("spa", 1, sz.PS), ("red", C, sz.PW)):
+    for name, z, part, width in (("exp", C, sz.PW, wp), ("spa", 1, sz.PS, K), ("red", C, sz.PW, wp)):
         table += [
-            (name + "_gs", (2, Q, z, part, LANES), BF16),
-            (name + "_rb", (Q, z, part, LANES), BF16),
-            (name + "_sm", (Q, z, part, LANES), BF16),
-            (name + "_rq", (Q, z, part, LANES), BF16),
-            (name + "_tot", (z, part, LANES), BF16),
-            (name + "_fin", (2, Q, z, part, LANES), BF16),
+            (name + "_gs", (2, Q, z, part, width), BF16),
+            (name + "_rb", (Q, z, part, width), BF16),
+            (name + "_sm", (Q, z, part, width), BF16),
+            (name + "_rq", (Q, z, part, width), BF16),
+            (name + "_tot", (z, part, width), BF16),
+            (name + "_fin", (2, Q, z, part, width), BF16),
         ]
     return table
 
 
-N_INPUTS, N_OUTPUTS = 8, 6
-
-
 def block_kernel(sz, *refs):
-    groups, images, cotangent, reduce_w, spatial_w, expand_w, inner_norm, outer_norm = refs[:8]
-    out_hbm, ing_hbm, exp_hbm, spa_hbm, red_hbm, small_out = refs[8:14]
+    groups, images, cotangent, inner_norm, outer_norm, inner_moments, outer_moments, inner_ema, outer_ema = refs[:9]
+    states_hbm = [refs[9:12], refs[12:15], refs[15:18]]
+    output, input_grad, red_state, spa_state, exp_state, inner_state, outer_state = refs[18:25]
     table = scratch_table(sz)
-    v = {name: ref for (name, _, _), ref in zip(table, refs[14:])}
-    lsem, w1ssem, w1rsem, ssem, rsem = refs[14 + len(table) :]
+    v = {name: ref for (name, _, _), ref in zip(table, refs[25:])}
+    lsem, stsem, w1ssem, w1rsem, ssem, rsem = refs[25 + len(table) :]
     D, C, Q, I, K, KB, WB = sz.D, sz.C, sz.Q, sz.I, sz.K, sz.KB, sz.WB
     ip, wp, R, RS, RP = sz.ip, sz.wp, sz.R, sz.RS, sz.RP
     d = lax.axis_index("dp")
@@ -166,22 +165,34 @@
         wait_bytes(ref, rsem.at[sem_of[name]])
         sent.append((name, ref))
 
+    def sent_done(name):
+        for entry in [e for e in sent if e[0] == name]:
+            wait_bytes(entry[1], ssem.at[sem_of[name]])
+            sent.remove(entry)
+
     barrier = pltpu.get_barrier_semaphore()
     for j in zpeers:
         pl.semaphore_signal(barrier, inc=1, device_id=(d, j), device_id_type=MESH)
     for e in dpeers:
         pl.semaphore_signal(barrier, inc=1, device_id=(e, c), device_id_type=MESH)
 
-    xi, stage, omap, mask, xb, cotb = v["xi"], v["stage"], v["omap"], v["mask"], v["xb"], v["cotb"]
-    w1f, w1s, w1r, w2f, w2s, w2r, wfull = (v[n] for n in ("w1f", "w1s", "w1r", "w2f", "w2s", "w2r", "wfull"))
+    xi, coti, mask, xb, cotb = (v[n] for n in ("xi", "coti", "mask", "xb", "cotb"))
+    w1s, w1r, w2s, w2r, wfull = (v[n] for n in ("w1s", "w1r", "w2s", "w2r", "wfull"))
+    w1f, wsf, w2f = red_state.at[0], spa_state.at[0], exp_state.at[0]
     loads = [
-        pltpu.make_async_copy(reduce_w, w1f, lsem.at[0]),
+        pltpu.make_async_copy(states_hbm[0][0], w1f, lsem.at[0]),
         pltpu.make_async_copy(images, xi, lsem.at[1]),
-        pltpu.make_async_copy(expand_w, w2f, lsem.at[2]),
-        pltpu.make_async_copy(spatial_w, wfull.at[c, pl.ds(0, sz.NS)], lsem.at[3]),
+        pltpu.make_async_copy(states_hbm[2][0], w2f, lsem.at[2]),
+        pltpu.make_async_copy(states_hbm[1][0], wsf, lsem.at[3]),
+        pltpu.make_async_copy(cotangent, coti, lsem.at[4]),
     ]
     for load in loads:
         load.start()
+    state_loads = []
+    for s, state in enumerate((red_state, spa_state, exp_state)):
+        places = (state.at[pl.ds(1, 2)], state.at[3])
+        for part, place in enumerate(places):
+            state_loads.append(pltpu.make_async_copy(states_hbm[s][part + 1], place, stsem.at[2 * s + part]))
 
     def columns_of(ref, j):
         return ref[:, pl.ds(pl.multiple_of(j * wp, wp), wp)].astype(BF16)
@@ -212,40 +223,20 @@
         cells_here = cells_here + inside
     mask[R:RP, :] = jnp.zeros((RP - R, LANES), F32)
     count_here = jnp.sum(cells_here, axis=0, keepdims=True)
-    img_rows = round_up(PIX, 8)
-
-    def by_cell(src, dst):
-        for i in range(I):
-            values = src[i].astype(F32)
-            for l in range(WB):
-                stage[l, i * img_rows : i * img_rows + PIX, :] = values[:, l * LANES : (l + 1) * LANES]
-
-        def pair(s, carry):
-            for l in range(WB):
-                both = [stage[l, pl.ds(2 * s + e, I, stride=img_rows), :] for e in range(2)]
-                dst[pl.ds(pl.multiple_of(s * 2 * I, 2 * I), 2 * I), l * LANES : (l + 1) * LANES] = (
-                    jnp.concatenate(both, axis=0).astype(BF16)
-                )
+
+    def by_rows(src, dst):
+        full = R // CHUNK * CHUNK
+
+        def step(n, carry):
+            rows = pl.ds(pl.multiple_of(n * CHUNK, CHUNK), CHUNK)
+            dst[rows, :] = src[rows, :]
             return carry
 
-        lax.fori_loop(0, PIX // 2, pair, 0)
-        for l in range(WB):
-            last = stage[l, pl.ds(PIX - 1, I, stride=img_rows), :]
-            rest = jnp.zeros((RP - R, LANES), F32)
-            dst[R - I : RP, l * LANES : (l + 1) * LANES] = jnp.concatenate([last, rest], axis=0).astype(BF16)
-
-    def by_image(src, dst):
-        def cell(p, carry):
-            for l in range(WB):
-                stage[l, pl.ds(p, I, stride=img_rows), :] = src[
-                    pl.ds(pl.multiple_of(p * I, I), I), l * LANES : (l + 1) * LANES
-                ]
-            return carry
-
-        lax.fori_loop(0, PIX, cell, 0)
-        for i in range(I):
-            for l in range(WB):
-                dst[i, :, l * LANES : (l + 1) * LANES] = stage[l, i * img_rows : i * img_rows + PIX, :]
+        lax.fori_loop(0, R // CHUNK, step, 0)
+        if RP > full:
+            rest = [src[full:R, :].astype(F32)] if R > full else []
+            rest.append(jnp.zeros((RP - R, src.shape[1]), F32))
+            dst[full:RP, :] = jnp.concatenate(rest, axis=0).astype(BF16)
 
     def lanes(values, width):
         if width <= LANES:
@@ -282,9 +273,7 @@
         return jnp.concatenate(list(values) + [rest], axis=0)
 
     loads[1].wait()
-    by_cell(xi, xb)
-    load_cot = pltpu.make_async_copy(cotangent, xi, lsem.at[4])
-    load_cot.start()
+    by_rows(xi, xb)
 
     acc, p1s, p1r = v["acc"], v["p1s"], v["p1r"]
     for k in range(1, C):
@@ -299,9 +288,13 @@
     w2r[c] = columns_of(w2f, c)
     for j in zpeers:
         send("w2", w2s.at[j], w2r.at[c], (d, j))
-    load_cot.wait()
-    by_cell(xi, cotb)
+    loads[4].wait()
+    by_rows(coti, cotb)
     loads[3].wait()
+    for t in range(TAPS):
+        wfull[c, t * ip : (t + 1) * ip, :] = wsf[t].astype(BF16)
+    for load in state_loads:
+        load.start()
 
     def add_partials(name, recv):
         got(name, recv.at[pl.ds(0, C - 1), pl.ds(0, RS)])
@@ -368,7 +361,7 @@
         average, inverse, count = combine(bn, table)
         par[c] = rows_of(
             inverse, (mean - average) * inverse,
-            inner_norm[0, layer : layer + 1, :], inner_norm[1, layer : layer + 1, :],
+            inner_norm[layer : layer + 1, :], inner_norm[2 + layer : 3 + layer, :],
         )
         send_z(par_name, par)
         got_z(held_name, held, RS)
@@ -411,8 +404,7 @@
         return jnp.concatenate(pieces, axis=0).astype(BF16)
 
     def weight_of(j, tap):
-        pieces = [wfull[j, pl.ds(pl.multiple_of((tap * KB + kb) * ip, ip), ip), :] for kb in range(KB)]
-        return jnp.concatenate(pieces, axis=1)
+        return wfull[j, pl.ds(pl.multiple_of(tap * ip, ip), ip), :]
 
     fill_pad()
     acc[...] = jnp.zeros_like(acc)
@@ -433,7 +425,7 @@
     act2 = v["act2"]
     make_act(v2, pm2, act2)
 
-    third, og, wide, tg = v["third"], v["og"], v["wide"], v["tg"]
+    third, og, tg = v["third"], v["og"], v["tg"]
     got_z("w2", w2r)
     third[...] = nn(act2[...], w2r[...].reshape(K, wp))
     mean3, spread3 = moments(third, wp)
@@ -449,7 +441,8 @@
         third[rows, :] = normed
         summed = gain3 * normed + bias3 + xb[rows, :].astype(F32)
         s = sigmoid(summed)
-        wide[rows, :] = summed * s * m
+        here = summed * s * m
+        output[rows, :] = here
         grad = cotb[rows, :].astype(F32) * (s * (1.0 + summed * (1.0 - s))) * m
         og[rows, :] = grad
         return carry[0] + fold_rows(grad), carry[1] + fold_rows(grad * normed)
@@ -458,9 +451,6 @@
     sums = over_chunks(last_step, (zero_wp, zero_wp))
     st4[d] = rows_of(total_of(sums[0]), total_of(sums[1]))
     exchange_dp("bk3", st4)
-    by_image(wide, omap)
-    store_out = pltpu.make_async_copy(omap, out_hbm, lsem.at[5])
-    store_out.start()
     bias_grad3, gain_grad3 = sum_dp("bk3", st4)
     scale3 = inverse3 * gain3
 
@@ -470,7 +460,8 @@
 
     each_chunk(third_step)
 
-    p2s, p2r = v["p2s"], v["p2r"]
+    p2s, p2r = p1s, v["p2r"]
+    sent_done("pre1")
     for k in range(1, C):
         j = lax.rem(c - k + C, C)
         p2s[j] = nt(tg[...], w2r[j]).astype(BF16)
@@ -484,16 +475,24 @@
                 v[name + "_" + s] for s in ("gs", "rb", "sm", "rq", "tot", "fin")
             )
 
-        def put(self, zi, block, value):
-            row, end = block * ip, (block + 1) * ip
+        def pieces(self, first, rows):
+            row, end = first, first + rows
             while row < end:
                 owner = row // self.part
                 stop = min(end, (owner + 1) * self.part)
-                at = row - owner * self.part
-                self.gs[owner % 2, owner // 2, zi, at : at + stop - row, :] = value[
-                    row - block * ip : stop - block * ip, :
-                ]
+                yield owner, row - owner * self.part, row - first, stop - row
                 row = stop
+
+        def put(self, zi, first, value):
+            for owner, there, here, n in self.pieces(first, value.shape[0]):
+                self.gs[owner % 2, owner // 2, zi, there : there + n, :] = value[here : here + n, :]
+
+        def take(self, zi, first, rows):
+            found = [
+                self.fin[owner % 2, owner // 2, zi, there : there + n, :].astype(F32)
+                for owner, there, _, n in self.pieces(first, rows)
+            ]
+            return jnp.concatenate(found, axis=0)
 
         def pair(self):
             send(self.name + "core", self.gs.at[1 - h], self.rb, (sibling, c))
@@ -535,9 +534,7 @@
     spa_red = Reduction("spa", 1, sz.PS)
     red_red = Reduction("red", C, sz.PW)
     for j in range(C):
-        block = tn(act2[:, j * ip : (j + 1) * ip], tg[...]).astype(BF16)
-        for wb in range(WB):
-            exp_red.put(j, wb, block[:, wb * LANES : (wb + 1) * LANES])
+        exp_red.put(j, 0, tn(act2[:, j * ip : (j + 1) * ip], tg[...]).astype(BF16))
     exp_red.pair()
 
     add_partials("grad2", p2r)
@@ -573,9 +570,7 @@
 
     each_chunk(own_second)
     for tap in range(TAPS):
-        block = tn(sgo[...], cols[tap]).astype(BF16)
-        for kb in range(KB):
-            spa_red.put(0, tap * KB + kb, block[:, kb * LANES : (kb + 1) * LANES])
+        spa_red.put(0, tap * ip, tn(sgo[...], cols[tap]).astype(BF16))
     exp_red.chan()
     spa_red.pair()
     got_z("dlt2", d2b, RS)
@@ -634,54 +629,99 @@
 
     each_chunk(first_step)
     for j in range(C):
-        block = tn(fg[:, j * ip : (j + 1) * ip], xb[...]).astype(BF16)
-        for wb in range(WB):
-            red_red.put(j, wb, block[:, wb * LANES : (wb + 1) * LANES])
+        red_red.put(j, 0, tn(fg[:, j * ip : (j + 1) * ip], xb[...]).astype(BF16))
     red_red.pair()
-    wide[...] = nn(fg[...], w1r[...].reshape(K, wp)) + og[...]
+    input_grad[...] = nn(fg[...], w1r[...].reshape(K, wp)) + og[...]
     red_red.chips()
     spa_red.other()
+
+    def adam(state, at, grad, rate, decay):
+        weight, moment, square, average = (state[(part, *at)] for part in range(4))
+        first = beta_one * moment + (1.0 - beta_one) * grad
+        second = beta_two * square + (1.0 - beta_two) * grad * grad
+        scaled = first * (1.0 / (1.0 - beta_one**STEP))
+        root = jnp.sqrt(second * (1.0 / (1.0 - beta_two**STEP))) + adam_eps
+        updated = weight - rate * (scaled / root + decay * weight)
+        state[(0, *at)] = updated
+        state[(1, *at)] = first
+        state[(2, *at)] = second
+        state[(3, *at)] = ema_rate * average + (1.0 - ema_rate) * updated
+
+    def adam_rows(red, state, rate):
+        for j in range(C):
+            for first in range(0, ip, 32):
+                n = min(32, ip - first)
+                adam(state, (slice(first, first + n), slice(j * wp, (j + 1) * wp)), red.take(j, first, n), rate, decay_rate)
+
+    for load in state_loads:
+        load.wait()
+    red_red.chan()
     exp_red.done()
-    store_out.wait()
-    by_image(wide, omap)
-    store_in = pltpu.make_async_copy(omap, ing_hbm, lsem.at[6])
-    store_in.start()
-    red_red.chan()
+    adam_rows(exp_red, exp_state, 2.0 / math.sqrt(K))
     red_red.back()
-    store_exp = pltpu.make_async_copy(exp_red.fin, exp_hbm, lsem.at[7])
-    store_exp.start()
     spa_red.done()
-    store_spa = pltpu.make_async_copy(spa_red.fin, spa_hbm, lsem.at[8])
-    store_spa.start()
-    small_out[...] = jnp.zeros_like(small_out)
-    small_out[0:1, 0:K] = gain_grad1
-    small_out[1:2, 0:K] = bias_grad1
-    small_out[2:3, 0:ip] = gain_grad2
-    small_out[3:4, 0:ip] = bias_grad2
-    small_out[4:5, 0:wp] = gain_grad3
-    small_out[5:6, 0:wp] = bias_grad3
-    red_red.other()
+    for tap in range(TAPS):
+        for first in range(0, ip, 32):
+            n = min(32, ip - first)
+            adam(
+                spa_state, (tap, slice(first, first + n), slice(0, K)), spa_red.take(0, tap * ip + first, n),
+                2.0 / math.sqrt(TAPS * K), decay_rate,
+            )
+        if tap == TAPS // 2:
+            red_red.other()
+
+    own = v["own"]
+    for j in range(C):
+        own[j] = rows_of(gain_grad1[:, j * ip : (j + 1) * ip], bias_grad1[:, j * ip : (j + 1) * ip])
+    inner_grads = [own[c, 0:1, :], gain_grad2, own[c, 1:2, :], bias_grad2]
+    outer_grads = [gain_grad3, bias_grad3]
+    inner_state[0:4, :] = inner_norm[...]
+    for m in range(2):
+        for r in range(2):
+            inner_state[4 + 4 * m + 2 * r : 6 + 4 * m + 2 * r, :] = inner_moments[m, r]
+    inner_state[12:16, :] = inner_ema[...]
+    outer_state[0:2, :] = outer_norm[...]
+    outer_state[2:6, :] = outer_moments[...]
+    outer_state[6:8, :] = outer_ema[...]
+
+    def adam_small(state, n, grads):
+        grad = jnp.concatenate(grads, axis=0)
+        weight, moment, square, average = (state[part * n : (part + 1) * n, :] for part in range(4))
+        first = beta_one * moment + (1.0 - beta_one) * grad
+        second = beta_two * square + (1.0 - beta_two) * grad * grad
+        scaled = first * (1.0 / (1.0 - beta_one**STEP))
+        root = jnp.sqrt(second * (1.0 / (1.0 - beta_two**STEP))) + adam_eps
+        updated = weight - norm_rate * (scaled / root)
+        state[0:n, :] = updated
+        state[n : 2 * n, :] = first
+        state[2 * n : 3 * n, :] = second
+        state[3 * n : 4 * n, :] = ema_rate * average + (1.0 - ema_rate) * updated
+
+    adam_small(inner_state, 4, inner_grads)
+    adam_small(outer_state, 2, outer_grads)
     red_red.done()
-    store_red = pltpu.make_async_copy(red_red.fin, red_hbm, lsem.at[9])
-    store_red.start()
-    for copy in (store_in, store_exp, store_spa, store_red):
-        copy.wait()
+    adam_rows(red_red, red_state, 2.0 / math.sqrt(sz.W))
     for copy in w1_copies:
         copy.wait_send()
     for name, ref in sent:
         wait_bytes(ref, ssem.at[sem_of[name]])
 
 
-def adamw(weight, moments, average, grad, rate, decay):
-    first = beta_one * moments[0] + (1.0 - beta_one) * grad
-    second = beta_two * moments[1] + (1.0 - beta_two) * grad * grad
-    corr_one = 1.0 - beta_one**STEP
-    corr_two = 1.0 - beta_two**STEP
-    new_weight = weight - rate * (
-        first / corr_one / (jnp.sqrt(second / corr_two) + adam_eps) + decay * weight
-    )
-    new_average = ema_rate * average + (1.0 - ema_rate) * new_weight
-    return (new_weight, first, second, new_average)
+def store_kernel(n, *refs):
+    held, places, sem = refs[:7], refs[7 : 7 + n], refs[-1]
+    output, input_grad, red_state, spa_state, exp_state, inner_state, outer_state = held
+    parts = [output.at[pl.ds(0, places[0].shape[0])], input_grad.at[pl.ds(0, places[1].shape[0])]]
+    for state in (red_state, spa_state, exp_state):
+        parts += [state.at[part] for part in range(4)]
+    copies = [pltpu.make_async_copy(src, dst, sem.at[i]) for i, (src, dst) in enumerate(zip(parts, places))]
+    for copy in copies:
+        copy.start()
+    inner_places, outer_places = places[14:18], places[18:22]
+    for part in range(4):
+        inner_places[part][...] = inner_state[part * 4 : (part + 1) * 4, :]
+        outer_places[part][...] = outer_state[part * 2 : (part + 1) * 2, :]
+    for copy in copies:
+        copy.wait()
 
 
 def per_device(
@@ -691,59 +731,62 @@
     reduce_ema, spatial_ema, expand_ema, inner_ema, outer_ema,
 ):
     sz = Sizes(mesh_dp, mesh_chan, images, reduce_weight)
-    ip, K, D = sz.ip, sz.K, sz.D
-    spatial_low = (
-        spatial_weight.reshape(ip, TAPS * sz.KB, LANES).transpose(1, 0, 2).reshape(sz.NS, LANES).astype(BF16)
+    ip, wp, K, C = sz.ip, sz.wp, sz.K, sz.C
+
+    def by_cell(a):
+        return a.transpose(1, 0, 2).reshape(sz.R, wp)
+
+    def by_tap(a):
+        return a.transpose(1, 2, 0, 3).reshape(TAPS, ip, K)
+
+    any_spec, vmem_spec = pl.BlockSpec(memory_space=pl.ANY), pl.BlockSpec(memory_space=pltpu.VMEM)
+    states = []
+    for weight, moments, ema in (
+        (reduce_weight, reduce_moments, reduce_ema),
+        (by_tap(spatial_weight), spatial_moments.transpose(0, 2, 3, 1, 4).reshape(2, TAPS, ip, K), by_tap(spatial_ema)),
+        (expand_weight, expand_moments, expand_ema),
+    ):
+        states += [weight, moments, ema]
+    held_shapes = (
+        (sz.RP, wp), (sz.RP, wp), (4, ip, sz.W), (4, TAPS, ip, K), (4, ip, sz.W), (16, ip), (8, wp),
     )
-    wide_row = max(K, sz.wp)
-    any_spec, vmem_spec = pl.BlockSpec(memory_space=pl.ANY), pl.BlockSpec(memory_space=pltpu.VMEM)
-    output, input_grad, exp_sum, spa_sum, red_sum, small = pl.pallas_call(
+    held = pl.pallas_call(
         functools.partial(block_kernel, sz),
-        out_shape=(
-            jax.ShapeDtypeStruct(images.shape, F32),
-            jax.ShapeDtypeStruct(images.shape, F32),
-            jax.ShapeDtypeStruct((2, sz.Q, sz.C, sz.PW, LANES), BF16),
-            jax.ShapeDtypeStruct((2, sz.Q, 1, sz.PS, LANES), BF16),
-            jax.ShapeDtypeStruct((2, sz.Q, sz.C, sz.PW, LANES), BF16),
-            jax.ShapeDtypeStruct((8, wide_row), F32),
-        ),
-        in_specs=[pl.BlockSpec(memory_space=pltpu.SMEM)] + [any_spec] * 5 + [vmem_spec] * 2,
-        out_specs=(any_spec,) * 5 + (vmem_spec,),
+        out_shape=tuple(pltpu.VMEM(shape, F32) for shape in held_shapes),
+        in_specs=[pl.BlockSpec(memory_space=pltpu.SMEM)] + [any_spec] * 2 + [vmem_spec] * 6 + [any_spec] * 9,
+        out_specs=(vmem_spec,) * len(held_shapes),
         scratch_shapes=[pltpu.VMEM(shape, dtype) for _, shape, dtype in scratch_table(sz)]
         + [
-            pltpu.SemaphoreType.DMA((10,)),
-            pltpu.SemaphoreType.DMA((sz.C - 1,)),
-            pltpu.SemaphoreType.DMA((sz.C - 1,)),
+            pltpu.SemaphoreType.DMA((5,)),
+            pltpu.SemaphoreType.DMA((6,)),
+            pltpu.SemaphoreType.DMA((C - 1,)),
+            pltpu.SemaphoreType.DMA((C - 1,)),
             pltpu.SemaphoreType.DMA((len(PHASES),)),
             pltpu.SemaphoreType.DMA((len(PHASES),)),
         ],
         compiler_params=pltpu.CompilerParams(
-            collective_id=0, has_side_effects=True, vmem_limit_bytes=60 * 2**20
+            collective_id=0, has_side_effects=True, vmem_limit_bytes=VMEM_TOTAL - sum(vmem_bytes(shape, F32) for shape in held_shapes)
         ),
-    )(groups, images, cotangent, reduce_weight, spatial_low, expand_weight, inner_norm, outer_norm)
-
-    def whole(parts, z, n, cols):
-        rows = parts.transpose(2, 1, 0, 3, 4).reshape(z, -1, LANES)[:, :n]
-        rows = rows.reshape(z * n // ip, ip, LANES).transpose(1, 0, 2)
-        return rows.reshape(ip, cols).astype(F32)
-
-    exp_grad = whole(exp_sum, sz.C, sz.NW, sz.W)
-    red_grad = whole(red_sum, sz.C, sz.NW, sz.W)
-    spa_grad = whole(spa_sum, 1, sz.NS, TAPS * K).reshape(spatial_weight.shape)
-    own = lax.axis_index("chan") * ip
-    first_rows = lax.dynamic_slice(small[0:2, :K], (0, own), (2, ip))
-    inner_grad = jnp.stack(
-        [jnp.stack([first_rows[0], small[2, :ip]]), jnp.stack([first_rows[1], small[3, :ip]])]
+    )(
+        groups, by_cell(images), by_cell(cotangent),
+        inner_norm.reshape(4, ip), outer_norm, inner_moments, outer_moments.reshape(4, wp),
+        inner_ema.reshape(4, ip), outer_ema, *states,
     )
-    outer_grad = small[4:6, : sz.wp]
-    new_reduce = adamw(reduce_weight, reduce_moments, reduce_ema, red_grad, 2.0 / math.sqrt(sz.W), decay_rate)
-    new_spatial = adamw(
-        spatial_weight, spatial_moments, spatial_ema, spa_grad, 2.0 / math.sqrt(TAPS * K), decay_rate
-    )
-    new_expand = adamw(expand_weight, expand_moments, expand_ema, exp_grad, 2.0 / math.sqrt(K), decay_rate)
-    new_inner = adamw(inner_norm, inner_moments, inner_ema, inner_grad, norm_rate, 0.0)
-    new_outer = adamw(outer_norm, outer_moments, outer_ema, outer_grad, norm_rate, 0.0)
-    return (output, input_grad, *new_reduce, *new_spatial, *new_expand, *new_inner, *new_outer)
+    held = [pltpu.with_memory_space_constraint(a, pltpu.VMEM) for a in held]
+    shapes = [(sz.R, wp)] * 2 + [(ip, sz.W)] * 4 + [(TAPS, ip, K)] * 4 + [(ip, sz.W)] * 4
+    small = [(4, ip)] * 4 + [(2, wp)] * 4
+    results = pl.pallas_call(
+        functools.partial(store_kernel, len(shapes + small)),
+        out_shape=tuple(jax.ShapeDtypeStruct(shape, F32) for shape in shapes + small),
+        in_specs=[vmem_spec] * len(held),
+        out_specs=(any_spec,) * len(shapes) + (vmem_spec,) * len(small),
+        scratch_shapes=[pltpu.SemaphoreType.DMA((len(shapes),))],
+        compiler_params=pltpu.CompilerParams(vmem_limit_bytes=2 * 2**20),
+    )(*held)
+    images_of = [a.reshape(PIX, sz.I, wp).transpose(1, 0, 2) for a in results[:2]]
+    taps = [a.reshape(3, 3, ip, K).transpose(2, 0, 1, 3) for a in results[6:10]]
+    inner = [a.reshape(2, 2, ip) for a in results[14:18]]
+    return (*images_of, *results[2:6], *taps, *results[10:14], *inner, *results[18:22])
 
 
 def solution(mesh):

time: 301 us -> 198 us (0.66)
  local copies, waits for them, and re-layouts: 88.3 us -> 1.31 us
  other arithmetic: 22.7 us -> 0 us
  Pallas kernels: 188 us -> 196 us
    unnamed x56 -> x0, local copies, waits for them, and re-layouts: 64.7 us -> none
    add x5 -> x0, other arithmetic: 19.7 us -> none  [adamw(): new_average = ema_rate * average + (1.0 - ema_rate) * new_weight]
    convert_element_type x7 -> x0, local copies, waits for them, and re-layouts: 12.2 us -> none  [the longest x6 10.8 us: whole(): return rows.reshape(ip, cols).astype(F32)]
    slice x5 -> x0, local copies, waits for them, and re-layouts: 11.4 us -> none  [the longest x3 11.4 us: adamw(): second = beta_two * moments[1] + (1.0 - beta_two) * grad * grad]
    pallas_call x1 -> x2, Pallas kernels: 188 us -> 196 us  [the longest x1 188 us: per_device(): pl.pallas_call(functools.partial(block_kernel, sz), out_shape=tuple((pltp...]
    convert_element_type x3 -> x0, other arithmetic: 3.03 us -> none  [the longest x2 2.86 us: whole(): return rows.reshape(ip, cols).astype(F32)]
where the time goes in v2:
time: 198 us
  Pallas kernels  196 us (99%)
    pallas_call x1, Pallas kernels, per_device(): pl.pallas_call(functools.partial(block_kernel, sz), out_shape=tuple((pltp...  188 us
    pallas_call x1, Pallas kernels, per_device(): pl.pallas_call(functools.partial(store_kernel, len(shapes + small)), out_...  7.71 us

profile of v2, /device:TPU:0, one launch (start us, length us, event | category | flops | bytes accessed | tf_op | source)
XLA Modules:
  0.0 198.1 jit_solution(11248957505454573357)
XLA Ops:
  0.7 1.3 reshape.101.refs_6_
  2.0 188.2 %shard_map.345 = (f32[672,512]{1,0:T(8,128)S(1)}, f32[672,512]{1,0:T(8,128)S(1)}, f32[4,128,2048]{2,1,0:T(8,128)S(1)}, f32[4,9,128,512]{3,2,1,0:T(8,128)S(1)}, f...) custom-call(s32[8]{0:T(128)} %refs_0_.1, bf16[648,512]{1,0:T(8,128)(2,1)} %bitcast.42, ...), custom_call_target="tpu_custom_call" | custom-call | tf_op jit(solution)/shard_map/pallas_call | solution.py:753
  190.2 7.7 %shard_map.346 = (f32[648,512]{1,0:T(8,128)}, f32[648,512]{1,0:T(8,128)}, f32[128,2048]{1,0:T(8,128)}, f32[128,2048]{1,0:T(8,128)}, f32[128,2048]{1,0:T(8,128)},...) custom-call(f32[672,512]{1,0:T(8,128)S(1)} %get-tuple-element.51.ref, ...), custom_call_target="tpu_custom_call" | custom-call | tf_op jit(solution)/shard_map/pallas_call | solution.py:778

commit v3 on v2

--- a/solution.py
+++ b/solution.py
@@ -46,16 +46,22 @@
         self.R = PIX * self.I
         self.RS = round_up(self.R, 16)
         self.RP = round_up(self.R, CHUNK)
+        self.RT = 8 * CHUNK
         self.NS = TAPS * self.ip
         self.PW = round_up(-(-self.ip // self.D), 16)
         self.PS = round_up(-(-self.NS // self.D), 16)
         self.PADROWS = ((MAP + 2) * PITCH + 2) * self.I
 
 
-Z_PHASES = ["w2", "pre1", "act1", "par1", "act2", "par2", "grad2", "dlt2", "par3", "wsp", "zexp", "zred"]
-D_PHASES = ["bn1", "bn2", "bn3", "bk3", "bk2", "bk1", "wdp"]
-R_PHASES = [g + s for g in ("exp", "spa", "red") for s in ("core", "chip", "back", "pair")]
-PHASES = Z_PHASES + D_PHASES + R_PHASES
+Z_PHASES = ["w2", "pre1", "grad2", "wsp", "zexp", "zred"]
+Z_PHASES += [name + part for name in ("act1", "act2", "dlt2") for part in ("top", "par", "low")]
+D_PHASES = ["w2pair", "bn1", "bn2", "bn3", "bk3", "bk2", "bk1", "wchip", "wpair"]
+R_PHASES = [g + s for g in ("exp", "spa", "red") for s in ("core", "chip", "back0", "back1", "pair")]
+
+
+def phases(sz):
+    each = [name + str(k) for name in ("w1", "w1pair") for k in range(sz.C - 1)]
+    return Z_PHASES + D_PHASES + R_PHASES + each
 
 
 def nt(a, b):
@@ -94,7 +100,6 @@
         ("wfull", (C, D * sz.PS, K), BF16),
         ("p1s", (C, RP, ip), BF16),
         ("p1r", (C, RP, ip), BF16),
-        ("p2r", (C, RP, ip), BF16),
         ("v1", (C, RP, ip), BF16),
         ("v2", (C, RP, ip), BF16),
         ("d2b", (C, RP, ip), BF16),
@@ -138,7 +143,7 @@
     output, input_grad, red_state, spa_state, exp_state, inner_state, outer_state = refs[18:25]
     table = scratch_table(sz)
     v = {name: ref for (name, _, _), ref in zip(table, refs[25:])}
-    lsem, stsem, w1ssem, w1rsem, ssem, rsem = refs[25 + len(table) :]
+    lsem, stsem, ssem, rsem = refs[25 + len(table) :]
     D, C, Q, I, K, KB, WB = sz.D, sz.C, sz.Q, sz.I, sz.K, sz.KB, sz.WB
     ip, wp, R, RS, RP = sz.ip, sz.wp, sz.R, sz.RS, sz.RP
     d = lax.axis_index("dp")
@@ -149,7 +154,7 @@
     dpeers = [lax.rem(d + k, D) for k in range(1, D)]
     qpeers = [lax.rem(q + k, Q) for k in range(1, Q)]
     sibling = d + 1 - 2 * h
-    sem_of = {name: i for i, name in enumerate(PHASES)}
+    sem_of = {name: i for i, name in enumerate(phases(sz))}
     sent = []
 
     def send(name, src, dst, device):
@@ -202,15 +207,12 @@
         w1s[j] = columns_of(w1f, j)
     w1r[c] = columns_of(w1f, c)
     pl.semaphore_wait(barrier, C - 1 + D - 1)
-    w1_copies = []
+
+    def half(ref, j, side):
+        return ref.at[j, pl.ds(pl.multiple_of(side * (ip // 2), 16), ip // 2)]
+
     for k, j in enumerate(zpeers):
-        w1_copies.append(
-            pltpu.make_async_remote_copy(
-                src_ref=w1s.at[j], dst_ref=w1r.at[c], send_sem=w1ssem.at[k], recv_sem=w1rsem.at[k],
-                device_id=(d, j), device_id_type=MESH,
-            )
-        )
-        w1_copies[-1].start()
+        send("w1" + str(k), half(w1s, j, h), half(w1r, c, h), (d, j))
 
     row = lax.broadcasted_iota(jnp.int32, (I, LANES), 0)
     side = jnp.zeros((I, LANES), jnp.int32)
@@ -276,9 +278,12 @@
     by_rows(xi, xb)
 
     acc, p1s, p1r = v["acc"], v["p1s"], v["p1r"]
-    for k in range(1, C):
-        j = lax.rem(c - k + C, C)
-        w1_copies[k - 1].wait_recv()
+    sources = [lax.rem(c - k + C, C) for k in range(1, C)]
+    for k, j in enumerate(sources):
+        got("w1" + str(k), half(w1r, j, h))
+        send("w1pair" + str(k), half(w1r, j, h), half(w1r, j, h), (sibling, c))
+    for k, j in enumerate(sources):
+        got("w1pair" + str(k), half(w1r, j, 1 - h))
         p1s[j] = nt(xb[...], w1r[j]).astype(BF16)
         send("pre1", p1s.at[j, pl.ds(0, RS)], p1r.at[c, pl.ds(0, RS)], (d, j))
     acc[...] = nt(xb[...], w1r[c])
@@ -286,8 +291,6 @@
     for j in zpeers:
         w2s[j] = columns_of(w2f, j)
     w2r[c] = columns_of(w2f, c)
-    for j in zpeers:
-        send("w2", w2s.at[j], w2r.at[c], (d, j))
     loads[4].wait()
     by_rows(coti, cotb)
     loads[3].wait()
@@ -348,7 +351,28 @@
     def got_z(name, ref, rows=None):
         got(name, ref.at[pl.ds(0, C - 1)] if rows is None else ref.at[pl.ds(0, C - 1), pl.ds(0, rows)])
 
-    def inner_forward(layer, bn, table, held, held_name, par, par_name):
+    def joined(blocks, rows):
+        return jnp.concatenate([blocks[j, rows, :].astype(F32) for j in range(C)], axis=1)
+
+    def table_row(par, r):
+        return jnp.concatenate([par[j, r : r + 1, :] for j in range(C)], axis=1)
+
+    def own_part(values):
+        own = v["own"]
+        for j in range(C):
+            own[j, 0 : values.shape[0], :] = values[:, j * ip : (j + 1) * ip]
+        return own[c, 0 : values.shape[0], :]
+
+    top_rows, low_rows = pl.ds(0, sz.RT), pl.ds(sz.RT, RS - sz.RT)
+
+    def send_part(name, held, rows):
+        for j in zpeers:
+            send(name, held.at[c, rows], held.at[c, rows], (d, j))
+
+    def got_part(name, held, rows):
+        got(name, held.at[pl.ds(0, C - 1), rows])
+
+    def inner_forward(layer, bn, table, held, name, par):
         mean, spread = moments(acc, ip)
         table[d] = rows_of(mean, spread, lanes(count_here, ip))
         exchange_dp(bn, table)
@@ -357,28 +381,25 @@
             held[c, rows, :] = ((acc[rows, :] - mean) * mask_of(rows, ip)).astype(BF16)
 
         each_chunk(center)
-        send_z(held_name, held, RS)
+        send_part(name + "top", held, top_rows)
         average, inverse, count = combine(bn, table)
         par[c] = rows_of(
             inverse, (mean - average) * inverse,
             inner_norm[layer : layer + 1, :], inner_norm[2 + layer : 3 + layer, :],
         )
-        send_z(par_name, par)
-        got_z(held_name, held, RS)
-        got_z(par_name, par)
+        send_z(name + "par", par)
+        send_part(name + "low", held, low_rows)
+        got_part(name + "top", held, top_rows)
+        got_z(name + "par", par)
+        got_part(name + "low", held, low_rows)
         return count
-
-    def joined(blocks, rows):
-        return jnp.concatenate([blocks[j, rows, :].astype(F32) for j in range(C)], axis=1)
-
-    def table_row(par, r):
-        return jnp.concatenate([par[j, r : r + 1, :] for j in range(C)], axis=1)
 
     v1, v2, d2b, pm1, pm2, pm3 = (v[n] for n in ("v1", "v2", "d2b", "pm1", "pm2", "pm3"))
     for j in range(C):
         for ref in (v1, v2, d2b):
             ref[j, RS:RP, :] = jnp.zeros((RP - RS, ip), BF16)
-    count_ip = inner_forward(0, "bn1", v["st1"], v1, "act1", pm1, "par1")
+    count_ip = inner_forward(0, "bn1", v["st1"], v1, "act1", pm1)
+    count_k = lanes(lanes(count_ip, min(ip, LANES))[:, 0:1] + jnp.zeros((1, LANES), F32), K)
 
     def make_act(held, par, dst):
         inverse, shift, gain, bias = (table_row(par, r) for r in range(4))
@@ -389,6 +410,8 @@
 
         each_chunk(step)
 
+    for j in zpeers:
+        send("w2", half(w2s, j, h), half(w2r, c, h), (d, j))
     big, pad, cols = v["big"], v["pad"], v["cols"]
     pad[...] = jnp.zeros_like(pad)
     make_act(v1, pm1, big)
@@ -415,7 +438,10 @@
         return carry
 
     lax.fori_loop(0, TAPS, second_step, 0)
-    inner_forward(1, "bn2", v["st2"], v2, "act2", pm2, "par2")
+    got("w2", w2r.at[pl.ds(0, C - 1), pl.ds(0, ip // 2)])
+    for j in zpeers:
+        send("w2pair", half(w2r, j, h), half(w2r, j, h), (sibling, c))
+    inner_forward(1, "bn2", v["st2"], v2, "act2", pm2)
 
     def part_of(j, e):
         return wfull.at[j, pl.ds(pl.multiple_of(e * sz.PS, 16), sz.PS)]
@@ -426,7 +452,7 @@
     make_act(v2, pm2, act2)
 
     third, og, tg = v["third"], v["og"], v["tg"]
-    got_z("w2", w2r)
+    got("w2pair", w2r.at[pl.ds(0, C - 1), pl.ds(0, ip // 2)])
     third[...] = nn(act2[...], w2r[...].reshape(K, wp))
     mean3, spread3 = moments(third, wp)
     st3, st4, st5, st6 = v["st3"], v["st4"], v["st5"], v["st6"]
@@ -460,7 +486,12 @@
 
     each_chunk(third_step)
 
-    p2s, p2r = p1s, v["p2r"]
+    got("wsp", wfull.at[pl.ds(0, C - 1), pl.ds(0, sz.PS)])
+    for j in zpeers:
+        for e in qpeers:
+            send("wchip", part_of(j, d), part_of(j, d), (2 * e + h, c))
+
+    p2s, p2r = p1s, p1r
     sent_done("pre1")
     for k in range(1, C):
         j = lax.rem(c - k + C, C)
@@ -517,14 +548,24 @@
                 for j in zpeers:
                     send("z" + self.name, self.tot.at[j], self.fin.at[h, q, c], (d, j))
 
-        def back(self):
-            if self.z > 1:
+        def halves(self, side, other):
+            cut = round_up(self.part // 2, 16)
+            rows = pl.ds(0, cut) if side == 0 else pl.ds(cut, self.part - cut)
+            return self.fin.at[h, other, slice(None), rows]
+
+        def back(self, side):
+            if side == 0 and self.z > 1:
                 got("z" + self.name, self.fin.at[h, q, pl.ds(0, C - 1)])
+            if side == 1 and self.part <= 16:
+                return
             for e in qpeers:
-                send(self.name + "back", self.fin.at[h, q], self.fin.at[h, q], (2 * e + h, c))
+                send(self.name + "back" + str(side), self.halves(side, q), self.halves(side, q), (2 * e + h, c))
 
         def other(self):
-            got(self.name + "back", self.fin.at[h, pl.ds(0, Q - 1)])
+            cut = round_up(self.part // 2, 16)
+            got(self.name + "back0", self.fin.at[h, pl.ds(0, Q - 1), slice(None), pl.ds(0, cut)])
+            if self.part > 16:
+                got(self.name + "back1", self.fin.at[h, pl.ds(0, Q - 1), slice(None), pl.ds(cut, self.part - cut)])
             send(self.name + "pair", self.fin.at[h], self.fin.at[h], (sibling, c))
 
         def done(self):
@@ -552,15 +593,12 @@
     sums = over_chunks(second_back, (zero_ip, zero_ip))
     st5[d] = rows_of(total_of(sums[0]), total_of(sums[1]))
     exchange_dp("bk2", st5)
-    send_z("dlt2", d2b, RS)
+    send_part("dlt2top", d2b, top_rows)
+    bias_own2, gain_own2 = sum_dp("bk2", st5)
+    pm3[c] = rows_of(bias_own2 / count_ip, gain_own2 / count_ip)
+    send_z("dlt2par", pm3)
+    send_part("dlt2low", d2b, low_rows)
     exp_red.chips()
-    got("wsp", wfull.at[pl.ds(0, C - 1), pl.ds(0, sz.PS)])
-    for j in zpeers:
-        for e in dpeers:
-            send("wdp", part_of(j, d), part_of(j, d), (e, c))
-    bias_grad2, gain_grad2 = sum_dp("bk2", st5)
-    pm3[c] = rows_of(bias_grad2 / count_ip, gain_grad2 / count_ip)
-    send_z("par3", pm3)
     sgo = v["sgo"]
 
     def own_second(rows):
@@ -571,10 +609,16 @@
     each_chunk(own_second)
     for tap in range(TAPS):
         spa_red.put(0, tap * ip, tn(sgo[...], cols[tap]).astype(BF16))
+    spa_red.pair()
+    got("wchip", wfull.at[pl.ds(0, C - 1), pl.ds(0, (Q - 1) * sz.PS)])
+    for j in zpeers:
+        for e in range(Q):
+            send("wpair", part_of(j, 2 * e + h), part_of(j, 2 * e + h), (sibling, c))
     exp_red.chan()
-    spa_red.pair()
-    got_z("dlt2", d2b, RS)
-    got_z("par3", pm3)
+    spa_red.chips()
+    got_part("dlt2top", d2b, top_rows)
+    got_z("dlt2par", pm3)
+    got_part("dlt2low", d2b, low_rows)
     inverse2, shift2, gain2 = (table_row(pm2, r) for r in range(3))
     bias_part, gain_part = table_row(pm3, 0), table_row(pm3, 1)
     scale2 = inverse2 * gain2
@@ -586,54 +630,9 @@
 
     each_chunk(full_second)
     fill_pad()
-    spa_red.chips()
-    exp_red.back()
-    got("wdp", wfull.at[pl.ds(0, C - 1), pl.ds(0, (D - 1) * sz.PS)])
-
-    fag = v["fag"]
-    fag[...] = jnp.zeros_like(fag)
-
-    def first_act_step(tap, carry):
-        offset = ((2 - lax.div(tap, 3)) * PITCH + 2 - lax.rem(tap, 3)) * I
-        weight = jnp.concatenate([weight_of(j, tap) for j in range(C)], axis=0)
-        fag[...] += nn(shifted(offset), weight)
-        return carry
-
-    lax.fori_loop(0, TAPS, first_act_step, 0)
-    inverse1, shift1, gain1, bias1 = (table_row(pm1, r) for r in range(4))
-
-    def first_back(rows, carry):
-        normed = joined(v1, rows) * inverse1 + shift1
-        value = gain1 * normed + bias1
-        s = sigmoid(value)
-        grad = fag[rows, :] * (s * (1.0 + value * (1.0 - s))) * mask_of(rows, K)
-        fag[rows, :] = grad
-        big[rows, :] = normed
-        return carry[0] + fold_rows(grad), carry[1] + fold_rows(grad * normed)
-
-    zero_k = jnp.zeros((8, K), F32)
-    sums = over_chunks(first_back, (zero_k, zero_k))
-    st6[d] = rows_of(total_of(sums[0]), total_of(sums[1]))
-    exchange_dp("bk1", st6)
-    spa_red.chan()
-    spa_red.back()
-    exp_red.other()
-    bias_grad1, gain_grad1 = sum_dp("bk1", st6)
-    scale1 = inverse1 * gain1
-    count_k = lanes(count_ip[:, 0:1] + jnp.zeros((1, LANES), F32), K)
-    fg = v["fg"]
-
-    def first_step(rows):
-        back = mask_of(rows, K) * ((bias_grad1 + big[rows, :] * gain_grad1) / count_k)
-        fg[rows, :] = (scale1 * (fag[rows, :] - back)).astype(BF16)
-
-    each_chunk(first_step)
-    for j in range(C):
-        red_red.put(j, 0, tn(fg[:, j * ip : (j + 1) * ip], xb[...]).astype(BF16))
-    red_red.pair()
-    input_grad[...] = nn(fg[...], w1r[...].reshape(K, wp)) + og[...]
-    red_red.chips()
-    spa_red.other()
+    exp_red.back(0)
+    exp_red.back(1)
+    got("wpair", wfull.at[pl.ds(0, C - 1), pl.ds(0, Q * sz.PS)])
 
     def adam(state, at, grad, rate, decay):
         weight, moment, square, average = (state[(part, *at)] for part in range(4))
@@ -653,27 +652,75 @@
                 n = min(32, ip - first)
                 adam(state, (slice(first, first + n), slice(j * wp, (j + 1) * wp)), red.take(j, first, n), rate, decay_rate)
 
+    fag = v["fag"]
+    fag[...] = jnp.zeros_like(fag)
+
+    def first_act_step(tap, carry):
+        offset = ((2 - lax.div(tap, 3)) * PITCH + 2 - lax.rem(tap, 3)) * I
+        weight = jnp.concatenate([weight_of(j, tap) for j in range(C)], axis=0)
+        fag[...] += nn(shifted(offset), weight)
+        return carry
+
+    lax.fori_loop(0, TAPS // 2, first_act_step, 0)
+    exp_red.other()
+    lax.fori_loop(TAPS // 2, TAPS, first_act_step, 0)
+    inverse1, shift1, gain1, bias1 = (table_row(pm1, r) for r in range(4))
+
+    def first_back(rows, carry):
+        normed = joined(v1, rows) * inverse1 + shift1
+        value = gain1 * normed + bias1
+        s = sigmoid(value)
+        grad = fag[rows, :] * (s * (1.0 + value * (1.0 - s))) * mask_of(rows, K)
+        fag[rows, :] = grad
+        big[rows, :] = normed
+        return carry[0] + fold_rows(grad), carry[1] + fold_rows(grad * normed)
+
+    zero_k = jnp.zeros((8, K), F32)
+    sums = over_chunks(first_back, (zero_k, zero_k))
+    st6[d] = rows_of(total_of(sums[0]), total_of(sums[1]))
+    exchange_dp("bk1", st6)
+    spa_red.chan()
     for load in state_loads:
         load.wait()
-    red_red.chan()
     exp_red.done()
     adam_rows(exp_red, exp_state, 2.0 / math.sqrt(K))
-    red_red.back()
+    bias_grad1, gain_grad1 = sum_dp("bk1", st6)
+    scale1 = inverse1 * gain1
+    spa_red.back(0)
+    fg = v["fg"]
+
+    def first_step(rows):
+        back = mask_of(rows, K) * ((bias_grad1 + big[rows, :] * gain_grad1) / count_k)
+        fg[rows, :] = (scale1 * (fag[rows, :] - back)).astype(BF16)
+
+    each_chunk(first_step)
+    for j in range(C):
+        red_red.put(j, 0, tn(fg[:, j * ip : (j + 1) * ip], xb[...]).astype(BF16))
+    red_red.pair()
+    input_grad[...] = nn(fg[...], w1r[...].reshape(K, wp)) + og[...]
+    red_red.chips()
+
+    def adam_spatial(first_tap, last_tap):
+        for tap in range(first_tap, last_tap):
+            for first in range(0, ip, 32):
+                n = min(32, ip - first)
+                adam(
+                    spa_state, (tap, slice(first, first + n), slice(0, K)), spa_red.take(0, tap * ip + first, n),
+                    2.0 / math.sqrt(TAPS * K), decay_rate,
+                )
+
+    red_red.chan()
+    spa_red.back(1)
+    spa_red.other()
+    red_red.back(0)
+    red_red.back(1)
     spa_red.done()
-    for tap in range(TAPS):
-        for first in range(0, ip, 32):
-            n = min(32, ip - first)
-            adam(
-                spa_state, (tap, slice(first, first + n), slice(0, K)), spa_red.take(0, tap * ip + first, n),
-                2.0 / math.sqrt(TAPS * K), decay_rate,
-            )
-        if tap == TAPS // 2:
-            red_red.other()
-
-    own = v["own"]
-    for j in range(C):
-        own[j] = rows_of(gain_grad1[:, j * ip : (j + 1) * ip], bias_grad1[:, j * ip : (j + 1) * ip])
-    inner_grads = [own[c, 0:1, :], gain_grad2, own[c, 1:2, :], bias_grad2]
+    adam_spatial(0, TAPS // 2)
+    red_red.other()
+    adam_spatial(TAPS // 2, TAPS)
+
+    first_grads = own_part(jnp.concatenate([gain_grad1, bias_grad1], axis=0))
+    inner_grads = [first_grads[0:1, :], gain_own2, first_grads[1:2, :], bias_own2]
     outer_grads = [gain_grad3, bias_grad3]
     inner_state[0:4, :] = inner_norm[...]
     for m in range(2):
@@ -701,8 +748,6 @@
     adam_small(outer_state, 2, outer_grads)
     red_red.done()
     adam_rows(red_red, red_state, 2.0 / math.sqrt(sz.W))
-    for copy in w1_copies:
-        copy.wait_send()
     for name, ref in sent:
         wait_bytes(ref, ssem.at[sem_of[name]])
 
@@ -759,10 +804,8 @@
         + [
             pltpu.SemaphoreType.DMA((5,)),
             pltpu.SemaphoreType.DMA((6,)),
-            pltpu.SemaphoreType.DMA((C - 1,)),
-            pltpu.SemaphoreType.DMA((C - 1,)),
-            pltpu.SemaphoreType.DMA((len(PHASES),)),
-            pltpu.SemaphoreType.DMA((len(PHASES),)),
+            pltpu.SemaphoreType.DMA((len(phases(sz)),)),
+            pltpu.SemaphoreType.DMA((len(phases(sz)),)),
         ],
         compiler_params=pltpu.CompilerParams(
             collective_id=0, has_side_effects=True, vmem_limit_bytes=VMEM_TOTAL - sum(vmem_bytes(shape, F32) for shape in held_shapes)

time: 198 us -> 160 us (0.81)
  Pallas kernels: 196 us -> 157 us
    pallas_call x1, Pallas kernels: 188 us -> 150 us  [per_device(): pl.pallas_call(functools.partial(block_kernel, sz), out_shape=tuple((pltp...]
where the time goes in v3:
time: 160 us; the launch traced here: 159 us
  Pallas kernels  157 us (98%)
    pallas_call x1, Pallas kernels, per_device(): pl.pallas_call(functools.partial(block_kernel, sz), out_shape=tuple((pltp...  150 us
    pallas_call x1, Pallas kernels, per_device(): pl.pallas_call(functools.partial(store_kernel, len(shapes + small)), out_...  7.71 us

profile of v3, /device:TPU:0, one launch (start us, length us, event | category | flops | bytes accessed | tf_op | source)
XLA Modules:
  0.0 159.5 jit_solution(15079983649861347884)
XLA Ops:
  0.7 1.3 reshape.101.refs_6_
  2.0 149.6 %shard_map.345 = (f32[672,512]{1,0:T(8,128)S(1)}, f32[672,512]{1,0:T(8,128)S(1)}, f32[4,128,2048]{2,1,0:T(8,128)S(1)}, f32[4,9,128,512]{3,2,1,0:T(8,128)S(1)}, f...) custom-call(s32[8]{0:T(128)} %refs_0_.1, bf16[648,512]{1,0:T(8,128)(2,1)} %bitcast.42, ...), custom_call_target="tpu_custom_call" | custom-call | tf_op jit(solution)/shard_map/pallas_call | solution.py:798
  151.6 7.7 %shard_map.346 = (f32[648,512]{1,0:T(8,128)}, f32[648,512]{1,0:T(8,128)}, f32[128,2048]{1,0:T(8,128)}, f32[128,2048]{1,0:T(8,128)}, f32[128,2048]{1,0:T(8,128)},...) custom-call(f32[672,512]{1,0:T(8,128)S(1)} %get-tuple-element.51.ref, ...), custom_call_target="tpu_custom_call" | custom-call | tf_op jit(solution)/shard_map/pallas_call | solution.py:821

commit v4 on v3

--- a/solution.py
+++ b/solution.py
@@ -16,6 +16,7 @@
 STEP = 5
 LANES = 128
 CHUNK = 48
+CELLS_TOP = 4
 VMEM_TOTAL = 62 * 2**20
 
 norm_eps = 1e-05
@@ -53,14 +54,14 @@
         self.PADROWS = ((MAP + 2) * PITCH + 2) * self.I
 
 
-Z_PHASES = ["w2", "pre1", "grad2", "wsp", "zexp", "zred"]
+Z_PHASES = ["w2", "pre1", "grad2", "zexp", "zred"]
 Z_PHASES += [name + part for name in ("act1", "act2", "dlt2") for part in ("top", "par", "low")]
-D_PHASES = ["w2pair", "bn1", "bn2", "bn3", "bk3", "bk2", "bk1", "wchip", "wpair"]
+D_PHASES = ["w2chip", "w2pair", "bn1", "bn2", "bn3", "bk3", "bk2", "bk1"]
 R_PHASES = [g + s for g in ("exp", "spa", "red") for s in ("core", "chip", "back0", "back1", "pair")]
 
 
 def phases(sz):
-    each = [name + str(k) for name in ("w1", "w1pair") for k in range(sz.C - 1)]
+    each = [name + str(k) for name in ("w1", "w1pair", "wsp", "wchip0", "wchip1", "wpair") for k in range(sz.C - 1)]
     return Z_PHASES + D_PHASES + R_PHASES + each
 
 
@@ -95,8 +96,8 @@
         ("cotb", (RP, wp), BF16),
         ("w1s", (C, ip, wp), BF16),
         ("w1r", (C, ip, wp), BF16),
-        ("w2s", (C, ip, wp), BF16),
-        ("w2r", (C, ip, wp), BF16),
+        ("w2s", (C, D * sz.PW, wp), BF16),
+        ("w2r", (C, D * sz.PW, wp), BF16),
         ("wfull", (C, D * sz.PS, K), BF16),
         ("p1s", (C, RP, ip), BF16),
         ("p1r", (C, RP, ip), BF16),
@@ -127,8 +128,10 @@
     ]
     for name, z, part, width in (("exp", C, sz.PW, wp), ("spa", 1, sz.PS, K), ("red", C, sz.PW, wp)):
         table += [
-            (name + "_gs", (2, Q, z, part, width), BF16),
-            (name + "_rb", (Q, z, part, width), BF16),
+            *([] if name == "red" else [
+                (name + "_gs", (2, Q, z, part, width), BF16),
+                (name + "_rb", (Q, z, part, width), BF16),
+            ]),
             (name + "_sm", (Q, z, part, width), BF16),
             (name + "_rq", (Q, z, part, width), BF16),
             (name + "_tot", (z, part, width), BF16),
@@ -248,18 +251,20 @@
     def mask_of(rows, width):
         return lanes(mask[rows, :], width)
 
-    def over_chunks(body, carry=0):
+    everywhere, top_part, low_part = (0, RP // CHUNK), (0, sz.RT // CHUNK), (sz.RT // CHUNK, RP // CHUNK)
+
+    def over_chunks(body, carry=0, part=everywhere):
         def step(s, carry):
             return body(pl.ds(pl.multiple_of(s * CHUNK, CHUNK), CHUNK), carry)
 
-        return lax.fori_loop(0, RP // CHUNK, step, carry)
-
-    def each_chunk(body):
+        return lax.fori_loop(*part, step, carry)
+
+    def each_chunk(body, part=everywhere):
         def step(rows, carry):
             body(rows)
             return carry
 
-        over_chunks(step)
+        over_chunks(step, part=part)
 
     def fold_rows(values):
         total = values[0:8]
@@ -289,8 +294,8 @@
     acc[...] = nt(xb[...], w1r[c])
     loads[2].wait()
     for j in zpeers:
-        w2s[j] = columns_of(w2f, j)
-    w2r[c] = columns_of(w2f, c)
+        w2s[j, 0:ip, :] = columns_of(w2f, j)
+    w2r[c, 0:ip, :] = columns_of(w2f, c)
     loads[4].wait()
     by_rows(coti, cotb)
     loads[3].wait()
@@ -298,6 +303,40 @@
         wfull[c, t * ip : (t + 1) * ip, :] = wsf[t].astype(BF16)
     for load in state_loads:
         load.start()
+
+    def share(ref, j, e, n):
+        return ref.at[j, pl.ds(pl.multiple_of(e * n, 16), n)]
+
+    def part_of(j, e):
+        return share(wfull, j, e, sz.PS)
+
+    def fetch_spatial(k):
+        send("wsp" + str(k), part_of(c, d), part_of(c, d), (d, zpeers[k]))
+
+    cut = round_up(sz.PS // 2, 16)
+
+    def part_side(j, e, side):
+        start = pl.multiple_of(e * sz.PS + side * cut, 16)
+        return wfull.at[j, pl.ds(start, cut if side == 0 else sz.PS - cut)]
+
+    def spread_chips(k, side):
+        j = sources[k]
+        if side == 0:
+            got("wsp" + str(k), part_of(j, d))
+        for e in qpeers:
+            send("wchip" + str(side) + str(k), part_side(j, d, side), part_side(j, d, side), (2 * e + h, c))
+
+    def spread_pair(k):
+        j = sources[k]
+        got("wchip0" + str(k), wfull.at[j, pl.ds(0, (Q - 1) * cut)])
+        got("wchip1" + str(k), wfull.at[j, pl.ds(0, (Q - 1) * (sz.PS - cut))])
+        for e in range(Q):
+            send("wpair" + str(k), part_of(j, 2 * e + h), part_of(j, 2 * e + h), (sibling, c))
+
+    def spread_done(k):
+        got("wpair" + str(k), wfull.at[0, pl.ds(0, Q * sz.PS)])
+
+    late = list(reversed(range(1, C - 1)))
 
     def add_partials(name, recv):
         got(name, recv.at[pl.ds(0, C - 1), pl.ds(0, RS)])
@@ -372,7 +411,7 @@
     def got_part(name, held, rows):
         got(name, held.at[pl.ds(0, C - 1), rows])
 
-    def inner_forward(layer, bn, table, held, name, par):
+    def inner_forward(layer, bn, table, held, name, par, top_work, low_work, meanwhile=lambda: None):
         mean, spread = moments(acc, ip)
         table[d] = rows_of(mean, spread, lanes(count_here, ip))
         exchange_dp(bn, table)
@@ -389,71 +428,107 @@
         )
         send_z(name + "par", par)
         send_part(name + "low", held, low_rows)
+        meanwhile()
         got_part(name + "top", held, top_rows)
         got_z(name + "par", par)
+        top_work()
         got_part(name + "low", held, low_rows)
+        low_work()
         return count
 
     v1, v2, d2b, pm1, pm2, pm3 = (v[n] for n in ("v1", "v2", "d2b", "pm1", "pm2", "pm3"))
     for j in range(C):
         for ref in (v1, v2, d2b):
             ref[j, RS:RP, :] = jnp.zeros((RP - RS, ip), BF16)
-    count_ip = inner_forward(0, "bn1", v["st1"], v1, "act1", pm1)
-    count_k = lanes(lanes(count_ip, min(ip, LANES))[:, 0:1] + jnp.zeros((1, LANES), F32), K)
-
-    def make_act(held, par, dst):
+    def make_act(held, par, dst, part):
         inverse, shift, gain, bias = (table_row(par, r) for r in range(4))
 
         def step(rows):
             value = gain * (joined(held, rows) * inverse + shift) + bias
             dst[rows, :] = (value * sigmoid(value) * mask_of(rows, K)).astype(dst.dtype)
 
-        each_chunk(step)
-
-    for j in zpeers:
-        send("w2", half(w2s, j, h), half(w2r, c, h), (d, j))
+        each_chunk(step, part)
+
     big, pad, cols = v["big"], v["pad"], v["cols"]
     pad[...] = jnp.zeros_like(pad)
-    make_act(v1, pm1, big)
-
-    def fill_pad():
-        for y in range(MAP):
+    top_cells, low_cells = range(CELLS_TOP + 1), range(CELLS_TOP + 1, MAP)
+    top_out, low_out = range(CELLS_TOP), range(CELLS_TOP, MAP)
+
+    def fill_pad(cells):
+        for y in cells:
             start = ((y + 1) * PITCH + 1) * I
             pad[start : start + MAP * I, :] = big[y * MAP * I : (y + 1) * MAP * I, :]
 
-    def shifted(offset):
-        pieces = [pad[pl.ds(pl.multiple_of(offset + y * PITCH * I, I), MAP * I), :] for y in range(MAP)]
-        pieces.append(jnp.zeros((RP - R, K), F32))
+    def out_rows(cells):
+        return slice(0, CELLS_TOP * MAP * I) if cells is top_out else slice(CELLS_TOP * MAP * I, RP)
+
+    def shifted(offset, cells):
+        pieces = [pad[pl.ds(pl.multiple_of(offset + y * PITCH * I, I), MAP * I), :] for y in cells]
+        if cells is low_out:
+            pieces.append(jnp.zeros((RP - R, K), F32))
         return jnp.concatenate(pieces, axis=0).astype(BF16)
 
     def weight_of(j, tap):
         return wfull[j, pl.ds(pl.multiple_of(tap * ip, ip), ip), :]
 
-    fill_pad()
-    acc[...] = jnp.zeros_like(acc)
-
-    def second_step(tap, carry):
-        cols[tap] = shifted((lax.div(tap, 3) * PITCH + lax.rem(tap, 3)) * I)
-        acc[...] += nt(cols[tap], weight_of(c, tap))
-        return carry
-
-    lax.fori_loop(0, TAPS, second_step, 0)
-    got("w2", w2r.at[pl.ds(0, C - 1), pl.ds(0, ip // 2)])
-    for j in zpeers:
-        send("w2pair", half(w2r, j, h), half(w2r, j, h), (sibling, c))
-    inner_forward(1, "bn2", v["st2"], v2, "act2", pm2)
-
-    def part_of(j, e):
-        return wfull.at[j, pl.ds(pl.multiple_of(e * sz.PS, 16), sz.PS)]
-
-    for j in zpeers:
-        send("wsp", part_of(c, d), part_of(c, d), (d, j))
+    def second_conv(cells):
+        rows = out_rows(cells)
+        acc[rows, :] = jnp.zeros((rows.stop - rows.start, ip), F32)
+
+        def second_step(tap, carry):
+            cols[tap, rows, :] = shifted((lax.div(tap, 3) * PITCH + lax.rem(tap, 3)) * I, cells)
+            acc[rows, :] += nt(cols[tap, rows, :], weight_of(c, tap))
+            return carry
+
+        lax.fori_loop(0, TAPS, second_step, 0)
+
+    def first_top():
+        make_act(v1, pm1, big, top_part)
+        fill_pad(top_cells)
+        second_conv(top_out)
+
+    def first_low():
+        for j in zpeers:
+            send("w2", share(w2s, j, d, sz.PW), share(w2r, c, d, sz.PW), (d, j))
+        fetch_spatial(0)
+        make_act(v1, pm1, big, low_part)
+        fill_pad(low_cells)
+        second_conv(low_out)
+
+    count_ip = inner_forward(0, "bn1", v["st1"], v1, "act1", pm1, first_top, first_low)
+    count_k = lanes(lanes(count_ip, min(ip, LANES))[:, 0:1] + jnp.zeros((1, LANES), F32), K)
+
+    def hand_on():
+        got("w2", w2r.at[pl.ds(0, C - 1), pl.ds(0, sz.PW)])
+        for j in zpeers:
+            for e in qpeers:
+                send("w2chip", share(w2r, j, d, sz.PW), share(w2r, j, d, sz.PW), (2 * e + h, c))
+        spread_chips(0, 0)
+        spread_chips(0, 1)
+        got("w2chip", w2r.at[pl.ds(0, C - 1), pl.ds(0, (Q - 1) * sz.PW)])
+        for j in zpeers:
+            for e in range(Q):
+                send("w2pair", share(w2r, j, 2 * e + h, sz.PW), share(w2r, j, 2 * e + h, sz.PW), (sibling, c))
+        spread_pair(0)
+
     act2 = v["act2"]
-    make_act(v2, pm2, act2)
-
     third, og, tg = v["third"], v["og"], v["tg"]
-    got("w2pair", w2r.at[pl.ds(0, C - 1), pl.ds(0, ip // 2)])
-    third[...] = nn(act2[...], w2r[...].reshape(K, wp))
+
+    def third_conv(part):
+        make_act(v2, pm2, act2, part)
+        rows = slice(part[0] * CHUNK, part[1] * CHUNK)
+        third[rows, :] = nn(act2[rows, :], jnp.concatenate([w2r[j, 0:ip, :] for j in range(C)], axis=0))
+
+    def second_top():
+        got("w2pair", w2r.at[pl.ds(0, C - 1), pl.ds(0, Q * sz.PW)])
+        third_conv(top_part)
+
+    def second_low():
+        for k in late:
+            fetch_spatial(k)
+        third_conv(low_part)
+
+    inner_forward(1, "bn2", v["st2"], v2, "act2", pm2, second_top, second_low, hand_on)
     mean3, spread3 = moments(third, wp)
     st3, st4, st5, st6 = v["st3"], v["st4"], v["st5"], v["st6"]
     st3[d] = rows_of(mean3, spread3, lanes(count_here, wp))
@@ -486,24 +561,24 @@
 
     each_chunk(third_step)
 
-    got("wsp", wfull.at[pl.ds(0, C - 1), pl.ds(0, sz.PS)])
-    for j in zpeers:
-        for e in qpeers:
-            send("wchip", part_of(j, d), part_of(j, d), (2 * e + h, c))
-
     p2s, p2r = p1s, p1r
     sent_done("pre1")
     for k in range(1, C):
         j = lax.rem(c - k + C, C)
-        p2s[j] = nt(tg[...], w2r[j]).astype(BF16)
+        p2s[j] = nt(tg[...], w2r[j, 0:ip, :]).astype(BF16)
         send("grad2", p2s.at[j, pl.ds(0, RS)], p2r.at[c, pl.ds(0, RS)], (d, j))
-    acc[...] = nt(tg[...], w2r[c])
+    for k in late:
+        spread_chips(k, 0)
+        if k > 1:
+            spread_chips(k, 1)
+    acc[...] = nt(tg[...], w2r[c, 0:ip, :])
 
     class Reduction:
         def __init__(self, name, z, part):
             self.name, self.z, self.part = name, z, part
             self.gs, self.rb, self.sm, self.rq, self.tot, self.fin = (
-                v[name + "_" + s] for s in ("gs", "rb", "sm", "rq", "tot", "fin")
+                v[("exp" if name == "red" and s in ("gs", "rb") else name) + "_" + s]
+                for s in ("gs", "rb", "sm", "rq", "tot", "fin")
             )
 
         def pieces(self, first, rows):
@@ -571,69 +646,6 @@
         def done(self):
             got(self.name + "pair", self.fin.at[0])
 
-    exp_red = Reduction("exp", C, sz.PW)
-    spa_red = Reduction("spa", 1, sz.PS)
-    red_red = Reduction("red", C, sz.PW)
-    for j in range(C):
-        exp_red.put(j, 0, tn(act2[:, j * ip : (j + 1) * ip], tg[...]).astype(BF16))
-    exp_red.pair()
-
-    add_partials("grad2", p2r)
-    inverse_own, shift_own, gain_own, bias_own = (pm2[c, r : r + 1, :] for r in range(4))
-
-    def second_back(rows, carry):
-        normed = v2[c, rows, :].astype(F32) * inverse_own + shift_own
-        value = gain_own * normed + bias_own
-        s = sigmoid(value)
-        grad = acc[rows, :] * (s * (1.0 + value * (1.0 - s))) * mask_of(rows, ip)
-        d2b[c, rows, :] = grad.astype(BF16)
-        return carry[0] + fold_rows(grad), carry[1] + fold_rows(grad * normed)
-
-    zero_ip = jnp.zeros((8, ip), F32)
-    sums = over_chunks(second_back, (zero_ip, zero_ip))
-    st5[d] = rows_of(total_of(sums[0]), total_of(sums[1]))
-    exchange_dp("bk2", st5)
-    send_part("dlt2top", d2b, top_rows)
-    bias_own2, gain_own2 = sum_dp("bk2", st5)
-    pm3[c] = rows_of(bias_own2 / count_ip, gain_own2 / count_ip)
-    send_z("dlt2par", pm3)
-    send_part("dlt2low", d2b, low_rows)
-    exp_red.chips()
-    sgo = v["sgo"]
-
-    def own_second(rows):
-        normed = v2[c, rows, :].astype(F32) * inverse_own + shift_own
-        back = mask_of(rows, ip) * (pm3[c, 0:1, :] + normed * pm3[c, 1:2, :])
-        sgo[rows, :] = (inverse_own * gain_own * (d2b[c, rows, :].astype(F32) - back)).astype(BF16)
-
-    each_chunk(own_second)
-    for tap in range(TAPS):
-        spa_red.put(0, tap * ip, tn(sgo[...], cols[tap]).astype(BF16))
-    spa_red.pair()
-    got("wchip", wfull.at[pl.ds(0, C - 1), pl.ds(0, (Q - 1) * sz.PS)])
-    for j in zpeers:
-        for e in range(Q):
-            send("wpair", part_of(j, 2 * e + h), part_of(j, 2 * e + h), (sibling, c))
-    exp_red.chan()
-    spa_red.chips()
-    got_part("dlt2top", d2b, top_rows)
-    got_z("dlt2par", pm3)
-    got_part("dlt2low", d2b, low_rows)
-    inverse2, shift2, gain2 = (table_row(pm2, r) for r in range(3))
-    bias_part, gain_part = table_row(pm3, 0), table_row(pm3, 1)
-    scale2 = inverse2 * gain2
-
-    def full_second(rows):
-        normed = joined(v2, rows) * inverse2 + shift2
-        back = mask_of(rows, K) * (bias_part + normed * gain_part)
-        big[rows, :] = (scale2 * (joined(d2b, rows) - back)).astype(BF16).astype(F32)
-
-    each_chunk(full_second)
-    fill_pad()
-    exp_red.back(0)
-    exp_red.back(1)
-    got("wpair", wfull.at[pl.ds(0, C - 1), pl.ds(0, Q * sz.PS)])
-
     def adam(state, at, grad, rate, decay):
         weight, moment, square, average = (state[(part, *at)] for part in range(4))
         first = beta_one * moment + (1.0 - beta_one) * grad
@@ -652,18 +664,99 @@
                 n = min(32, ip - first)
                 adam(state, (slice(first, first + n), slice(j * wp, (j + 1) * wp)), red.take(j, first, n), rate, decay_rate)
 
+    exp_red = Reduction("exp", C, sz.PW)
+    spa_red = Reduction("spa", 1, sz.PS)
+    red_red = Reduction("red", C, sz.PW)
+    for j in range(C):
+        exp_red.put(j, 0, tn(act2[:, j * ip : (j + 1) * ip], tg[...]).astype(BF16))
+    exp_red.pair()
+
+    exp_red.chips()
+    for k in late[:-1]:
+        spread_pair(k)
+    exp_red.chan()
+    add_partials("grad2", p2r)
+    inverse_own, shift_own, gain_own, bias_own = (pm2[c, r : r + 1, :] for r in range(4))
+
+    def second_back(rows, carry):
+        normed = v2[c, rows, :].astype(F32) * inverse_own + shift_own
+        value = gain_own * normed + bias_own
+        s = sigmoid(value)
+        grad = acc[rows, :] * (s * (1.0 + value * (1.0 - s))) * mask_of(rows, ip)
+        d2b[c, rows, :] = grad.astype(BF16)
+        return carry[0] + fold_rows(grad), carry[1] + fold_rows(grad * normed)
+
+    zero_ip = jnp.zeros((8, ip), F32)
+    sums = over_chunks(second_back, (zero_ip, zero_ip))
+    st5[d] = rows_of(total_of(sums[0]), total_of(sums[1]))
+    exchange_dp("bk2", st5)
+    send_part("dlt2top", d2b, top_rows)
+    bias_own2, gain_own2 = sum_dp("bk2", st5)
+    pm3[c] = rows_of(bias_own2 / count_ip, gain_own2 / count_ip)
+    send_z("dlt2par", pm3)
+    send_part("dlt2low", d2b, low_rows)
+    for k in late[-1:]:
+        spread_chips(k, 1)
+    exp_red.back(0)
+    exp_red.back(1)
+    sgo = v["sgo"]
+
+    def own_second(rows):
+        normed = v2[c, rows, :].astype(F32) * inverse_own + shift_own
+        back = mask_of(rows, ip) * (pm3[c, 0:1, :] + normed * pm3[c, 1:2, :])
+        sgo[rows, :] = (inverse_own * gain_own * (d2b[c, rows, :].astype(F32) - back)).astype(BF16)
+
+    each_chunk(own_second)
+    for tap in range(TAPS):
+        spa_red.put(0, tap * ip, tn(sgo[...], cols[tap]).astype(BF16))
+    spa_red.pair()
+    for k in late[-1:]:
+        spread_pair(k)
+    exp_red.other()
+    spa_red.chips()
+    for load in state_loads:
+        load.wait()
+    exp_red.done()
+    adam_rows(exp_red, exp_state, 2.0 / math.sqrt(K))
     fag = v["fag"]
-    fag[...] = jnp.zeros_like(fag)
-
-    def first_act_step(tap, carry):
-        offset = ((2 - lax.div(tap, 3)) * PITCH + 2 - lax.rem(tap, 3)) * I
-        weight = jnp.concatenate([weight_of(j, tap) for j in range(C)], axis=0)
-        fag[...] += nn(shifted(offset), weight)
-        return carry
-
-    lax.fori_loop(0, TAPS // 2, first_act_step, 0)
-    exp_red.other()
-    lax.fori_loop(TAPS // 2, TAPS, first_act_step, 0)
+    inverse2, shift2, gain2 = (table_row(pm2, r) for r in range(3))
+    scale2 = inverse2 * gain2
+
+    def full_second(part):
+        bias_part, gain_part = table_row(pm3, 0), table_row(pm3, 1)
+
+        def step(rows):
+            normed = joined(v2, rows) * inverse2 + shift2
+            back = mask_of(rows, K) * (bias_part + normed * gain_part)
+            big[rows, :] = (scale2 * (joined(d2b, rows) - back)).astype(BF16).astype(F32)
+
+        each_chunk(step, part)
+
+    def first_act_grad(cells, first, last):
+        rows = out_rows(cells)
+        if first == 0:
+            fag[rows, :] = jnp.zeros((rows.stop - rows.start, K), F32)
+
+        def step(tap, carry):
+            offset = ((2 - lax.div(tap, 3)) * PITCH + 2 - lax.rem(tap, 3)) * I
+            weight = jnp.concatenate([weight_of(j, tap) for j in range(C)], axis=0)
+            fag[rows, :] += nn(shifted(offset, cells), weight)
+            return carry
+
+        lax.fori_loop(first, last, step, 0)
+
+    got_part("dlt2top", d2b, top_rows)
+    got_z("dlt2par", pm3)
+    full_second(top_part)
+    fill_pad(top_cells)
+    for k in range(C - 1):
+        spread_done(k)
+    first_act_grad(top_out, 0, TAPS)
+    got_part("dlt2low", d2b, low_rows)
+    full_second(low_part)
+    fill_pad(low_cells)
+    first_act_grad(low_out, 0, TAPS)
+
     inverse1, shift1, gain1, bias1 = (table_row(pm1, r) for r in range(4))
 
     def first_back(rows, carry):
@@ -680,13 +773,9 @@
     st6[d] = rows_of(total_of(sums[0]), total_of(sums[1]))
     exchange_dp("bk1", st6)
     spa_red.chan()
-    for load in state_loads:
-        load.wait()
-    exp_red.done()
-    adam_rows(exp_red, exp_state, 2.0 / math.sqrt(K))
     bias_grad1, gain_grad1 = sum_dp("bk1", st6)
+    spa_red.back(0)
     scale1 = inverse1 * gain1
-    spa_red.back(0)
     fg = v["fg"]
 
     def first_step(rows):
@@ -694,6 +783,7 @@
         fg[rows, :] = (scale1 * (fag[rows, :] - back)).astype(BF16)
 
     each_chunk(first_step)
+    sent_done("expcore")
     for j in range(C):
         red_red.put(j, 0, tn(fg[:, j * ip : (j + 1) * ip], xb[...]).astype(BF16))
     red_red.pair()

time: 160 us -> 153 us (0.956)
  Pallas kernels: 157 us -> 150 us
    pallas_call x1, Pallas kernels: 150 us -> 143 us  [per_device(): pl.pallas_call(functools.partial(block_kernel, sz), out_shape=tuple((pltp...]
where the time goes in v4:
time: 153 us; the launch traced here: 152 us
  Pallas kernels  150 us (98%)
    pallas_call x1, Pallas kernels, per_device(): pl.pallas_call(functools.partial(block_kernel, sz), out_shape=tuple((pltp...  143 us
    pallas_call x1, Pallas kernels, per_device(): pl.pallas_call(functools.partial(store_kernel, len(shapes + small)), out_...  7.71 us

profile of v4, /device:TPU:0, one launch (start us, length us, event | category | flops | bytes accessed | tf_op | source)
XLA Modules:
  0.0 152.5 jit_solution(6418283176682264429)
XLA Ops:
  0.7 1.3 reshape.101.refs_6_
  2.0 142.6 %shard_map.345 = (f32[672,512]{1,0:T(8,128)S(1)}, f32[672,512]{1,0:T(8,128)S(1)}, f32[4,128,2048]{2,1,0:T(8,128)S(1)}, f32[4,9,128,512]{3,2,1,0:T(8,128)S(1)}, f...) custom-call(s32[8]{0:T(128)} %refs_0_.1, bf16[648,512]{1,0:T(8,128)(2,1)} %bitcast.42, ...), custom_call_target="tpu_custom_call" | custom-call | tf_op jit(solution)/shard_map/pallas_call | solution.py:888
  144.6 7.7 %shard_map.346 = (f32[648,512]{1,0:T(8,128)}, f32[648,512]{1,0:T(8,128)}, f32[128,2048]{1,0:T(8,128)}, f32[128,2048]{1,0:T(8,128)}, f32[128,2048]{1,0:T(8,128)},...) custom-call(f32[672,512]{1,0:T(8,128)S(1)} %get-tuple-element.51.ref, ...), custom_call_target="tpu_custom_call" | custom-call | tf_op jit(solution)/shard_map/pallas_call | solution.py:911

commit v5 on v4

--- a/solution.py
+++ b/solution.py
@@ -16,7 +16,7 @@
 STEP = 5
 LANES = 128
 CHUNK = 48
-CELLS_TOP = 4
+CELLS_TOP = 2
 VMEM_TOTAL = 62 * 2**20
 
 norm_eps = 1e-05
@@ -47,7 +47,7 @@
         self.R = PIX * self.I
         self.RS = round_up(self.R, 16)
         self.RP = round_up(self.R, CHUNK)
-        self.RT = 8 * CHUNK
+        self.RT = 6 * CHUNK
         self.NS = TAPS * self.ip
         self.PW = round_up(-(-self.ip // self.D), 16)
         self.PS = round_up(-(-self.NS // self.D), 16)
@@ -110,10 +110,10 @@
         ("own", (C, 8, ip), F32),
         ("st1", (D, 8, ip), F32),
         ("st2", (D, 8, ip), F32),
-        ("st3", (D, 8, wp), F32),
-        ("st4", (D, 8, wp), F32),
+        ("st3", (D, 4, wp), F32),
+        ("st4", (D, 4, wp), F32),
         ("st5", (D, 8, ip), F32),
-        ("st6", (D, 8, K), F32),
+        ("st6", (D, 4, K), F32),
         ("acc", (RP, ip), F32),
         ("pad", (sz.PADROWS, K), F32),
         ("cols", (TAPS, RP, K), BF16),
@@ -276,7 +276,10 @@
         return jnp.sum(values, axis=0, keepdims=True)
 
     def rows_of(*values):
-        rest = jnp.zeros((8 - len(values), values[0].shape[1]), F32)
+        height = 8
+        if isinstance(values[0], int):
+            height, *values = values
+        rest = jnp.zeros((height - len(values), values[0].shape[1]), F32)
         return jnp.concatenate(list(values) + [rest], axis=0)
 
     loads[1].wait()
@@ -531,7 +534,7 @@
     inner_forward(1, "bn2", v["st2"], v2, "act2", pm2, second_top, second_low, hand_on)
     mean3, spread3 = moments(third, wp)
     st3, st4, st5, st6 = v["st3"], v["st4"], v["st5"], v["st6"]
-    st3[d] = rows_of(mean3, spread3, lanes(count_here, wp))
+    st3[d] = rows_of(4, mean3, spread3, lanes(count_here, wp))
     exchange_dp("bn3", st3)
     average3, inverse3, count_wp = combine("bn3", st3)
     gain3, bias3 = outer_norm[0:1, :], outer_norm[1:2, :]
@@ -550,7 +553,7 @@
 
     zero_wp = jnp.zeros((8, wp), F32)
     sums = over_chunks(last_step, (zero_wp, zero_wp))
-    st4[d] = rows_of(total_of(sums[0]), total_of(sums[1]))
+    st4[d] = rows_of(4, total_of(sums[0]), total_of(sums[1]))
     exchange_dp("bk3", st4)
     bias_grad3, gain_grad3 = sum_dp("bk3", st4)
     scale3 = inverse3 * gain3
@@ -674,7 +677,6 @@
     exp_red.chips()
     for k in late[:-1]:
         spread_pair(k)
-    exp_red.chan()
     add_partials("grad2", p2r)
     inverse_own, shift_own, gain_own, bias_own = (pm2[c, r : r + 1, :] for r in range(4))
 
@@ -697,8 +699,7 @@
     send_part("dlt2low", d2b, low_rows)
     for k in late[-1:]:
         spread_chips(k, 1)
-    exp_red.back(0)
-    exp_red.back(1)
+    exp_red.chan()
     sgo = v["sgo"]
 
     def own_second(rows):
@@ -712,12 +713,9 @@
     spa_red.pair()
     for k in late[-1:]:
         spread_pair(k)
-    exp_red.other()
     spa_red.chips()
     for load in state_loads:
         load.wait()
-    exp_red.done()
-    adam_rows(exp_red, exp_state, 2.0 / math.sqrt(K))
     fag = v["fag"]
     inverse2, shift2, gain2 = (table_row(pm2, r) for r in range(3))
     scale2 = inverse2 * gain2
@@ -755,6 +753,8 @@
     got_part("dlt2low", d2b, low_rows)
     full_second(low_part)
     fill_pad(low_cells)
+    exp_red.back(0)
+    exp_red.back(1)
     first_act_grad(low_out, 0, TAPS)
 
     inverse1, shift1, gain1, bias1 = (table_row(pm1, r) for r in range(4))
@@ -770,8 +770,9 @@
 
     zero_k = jnp.zeros((8, K), F32)
     sums = over_chunks(first_back, (zero_k, zero_k))
-    st6[d] = rows_of(total_of(sums[0]), total_of(sums[1]))
+    st6[d] = rows_of(4, total_of(sums[0]), total_of(sums[1]))
     exchange_dp("bk1", st6)
+    exp_red.other()
     spa_red.chan()
     bias_grad1, gain_grad1 = sum_dp("bk1", st6)
     spa_red.back(0)
@@ -804,6 +805,8 @@
     spa_red.other()
     red_red.back(0)
     red_red.back(1)
+    exp_red.done()
+    adam_rows(exp_red, exp_state, 2.0 / math.sqrt(K))
     spa_red.done()
     adam_spatial(0, TAPS // 2)
     red_red.other()

time: 153 us -> 149 us (0.974)
  Pallas kernels: 150 us -> 147 us
    pallas_call x1, Pallas kernels: 143 us -> 139 us  [per_device(): pl.pallas_call(functools.partial(block_kernel, sz), out_shape=tuple((pltp...]
where the time goes in v5:
time: 149 us
  Pallas kernels  147 us (99%)
    pallas_call x1, Pallas kernels, per_device(): pl.pallas_call(functools.partial(block_kernel, sz), out_shape=tuple((pltp...  139 us
    pallas_call x1, Pallas kernels, per_device(): pl.pallas_call(functools.partial(store_kernel, len(shapes + small)), out_...  7.71 us

profile of v5, /device:TPU:0, one launch (start us, length us, event | category | flops | bytes accessed | tf_op | source)
XLA Modules:
  0.0 149.0 jit_solution(10763925059499020296)
XLA Ops:
  0.7 1.3 reshape.101.refs_6_
  2.0 139.1 %shard_map.345 = (f32[672,512]{1,0:T(8,128)S(1)}, f32[672,512]{1,0:T(8,128)S(1)}, f32[4,128,2048]{2,1,0:T(8,128)S(1)}, f32[4,9,128,512]{3,2,1,0:T(8,128)S(1)}, f...) custom-call(s32[8]{0:T(128)} %refs_0_.1, bf16[648,512]{1,0:T(8,128)(2,1)} %bitcast.42, ...), custom_call_target="tpu_custom_call" | custom-call | tf_op jit(solution)/shard_map/pallas_call | solution.py:891
  141.1 7.7 %shard_map.346 = (f32[648,512]{1,0:T(8,128)}, f32[648,512]{1,0:T(8,128)}, f32[128,2048]{1,0:T(8,128)}, f32[128,2048]{1,0:T(8,128)}, f32[128,2048]{1,0:T(8,128)},...) custom-call(f32[672,512]{1,0:T(8,128)S(1)} %get-tuple-element.51.ref, ...), custom_call_target="tpu_custom_call" | custom-call | tf_op jit(solution)/shard_map/pallas_call | solution.py:914

commit v6 on v5

--- a/solution.py
+++ b/solution.py
@@ -47,7 +47,7 @@
         self.R = PIX * self.I
         self.RS = round_up(self.R, 16)
         self.RP = round_up(self.R, CHUNK)
-        self.RT = 6 * CHUNK
+        self.RT = 5 * CHUNK
         self.NS = TAPS * self.ip
         self.PW = round_up(-(-self.ip // self.D), 16)
         self.PS = round_up(-(-self.NS // self.D), 16)
@@ -155,6 +155,8 @@
     h = lax.rem(d, 2)
     zpeers = [lax.rem(c + k, C) for k in range(1, C)]
     dpeers = [lax.rem(d + k, D) for k in range(1, D)]
+    far_first = sorted(range(1, C), key=lambda k: -min(k, C - k))
+    far_first = [lax.rem(c + k, C) for k in far_first]
     qpeers = [lax.rem(q + k, Q) for k in range(1, Q)]
     sibling = d + 1 - 2 * h
     sem_of = {name: i for i, name in enumerate(phases(sz))}
@@ -566,8 +568,7 @@
 
     p2s, p2r = p1s, p1r
     sent_done("pre1")
-    for k in range(1, C):
-        j = lax.rem(c - k + C, C)
+    for j in far_first:
         p2s[j] = nt(tg[...], w2r[j, 0:ip, :]).astype(BF16)
         send("grad2", p2s.at[j, pl.ds(0, RS)], p2r.at[c, pl.ds(0, RS)], (d, j))
     for k in late:
@@ -802,9 +803,9 @@
 
     red_red.chan()
     spa_red.back(1)
-    spa_red.other()
     red_red.back(0)
     red_red.back(1)
+    spa_red.other()
     exp_red.done()
     adam_rows(exp_red, exp_state, 2.0 / math.sqrt(K))
     spa_red.done()

time: 149 us -> 149 us (level)
  no operation moved by 1% of the time
where the time goes in v6:
time: 149 us; the launch traced here: 148 us
  Pallas kernels  146 us (98%)
    pallas_call x1, Pallas kernels, per_device(): pl.pallas_call(functools.partial(block_kernel, sz), out_shape=tuple((pltp...  138 us
    pallas_call x1, Pallas kernels, per_device(): pl.pallas_call(functools.partial(store_kernel, len(shapes + small)), out_...  7.71 us

profile of v6, /device:TPU:0, one launch (start us, length us, event | category | flops | bytes accessed | tf_op | source)
XLA Modules:
  0.0 148.3 jit_solution(8532231817449164667)
XLA Ops:
  0.7 1.3 reshape.101.refs_6_
  2.0 138.5 %shard_map.345 = (f32[672,512]{1,0:T(8,128)S(1)}, f32[672,512]{1,0:T(8,128)S(1)}, f32[4,128,2048]{2,1,0:T(8,128)S(1)}, f32[4,9,128,512]{3,2,1,0:T(8,128)S(1)}, f...) custom-call(s32[8]{0:T(128)} %refs_0_.1, bf16[648,512]{1,0:T(8,128)(2,1)} %bitcast.42, ...), custom_call_target="tpu_custom_call" | custom-call | tf_op jit(solution)/shard_map/pallas_call | solution.py:892
  140.4 7.7 %shard_map.346 = (f32[648,512]{1,0:T(8,128)}, f32[648,512]{1,0:T(8,128)}, f32[128,2048]{1,0:T(8,128)}, f32[128,2048]{1,0:T(8,128)}, f32[128,2048]{1,0:T(8,128)},...) custom-call(f32[672,512]{1,0:T(8,128)S(1)} %get-tuple-element.51.ref, ...), custom_call_target="tpu_custom_call" | custom-call | tf_op jit(solution)/shard_map/pallas_call | solution.py:915
